TPU v7x, 32 devices: a whole 2x2x4 slice. The times are simulated.
32 devices in a mesh: grp: 2 (over y), seq: 4 (over z), head: 4 (over x, core).
Axes of the slice: x: 2, y: 2, z: 4, core: 2. Of those that a mesh axis runs over, the one named last changes fastest.
Arguments:
- q_heads: bfloat16 [8, 64, 16384], P('head', None, ('grp', 'seq')), parts along dimension 2, may hold values from -12 to 12
- k_heads: bfloat16 [8, 64, 16384], P('head', None, ('grp', 'seq')), parts along dimension 2, may hold values from -10 to 10
- v_heads: bfloat16 [8, 64, 16384], P('head', None, ('grp', 'seq')), parts along dimension 2, may hold values from -10 to 10
- morton_order: int32 [8, 2048], P(('grp', 'seq')), parts along dimension 0, may hold values from 0 to 2047, each once within a row
- leaf_counts: int32 [64], P('grp'), parts along dimension 0, may hold values from 64 to 256, as said below
Outputs:
- attended: bfloat16 [8, 64, 16384], P('head', None, ('grp', 'seq')), parts along dimension 2
There are 2 independent parts, one for each index of `grp`. A program takes and returns all parts, laid end to end along the dimension named above; each array names one. Nothing has to cross between parts.
Inputs may be any that keep to these rules, and one draw needn't show every extreme that they name: `morton_order`: each row holds every number of 0 .. 2047 once. `leaf_counts`: the valid points of a leaf are its first ones.
All inputs are finite; a program needn't handle non-finite values.
Results may differ from a plain program's by a relative error of at most 0.0021.
Values may be sent and summed in bfloat16 or wider, within the bound.
A program may use at most 64 MiB of HBM per device.

v0:
```python
import functools
import math

import jax
import jax.numpy as jnp
from jax import lax
from jax.experimental import pallas as pl
from jax.experimental.pallas import tpu as pltpu
from jax.sharding import PartitionSpec as P

LEAF = 256
NEG = -1e30
BF = jnp.bfloat16
F32 = jnp.float32
PAD = 16
BOUND = 10.0
STEPS = 32700.0
VMEM_LIMIT = 63 * 1024 * 1024 + 512 * 1024


def dot(a, b, dims=((1,), (0,))):
    return lax.dot_general(a, b, (dims, ((), ())), preferred_element_type=F32)


def split(x):
    hi = x.astype(BF)
    return hi, (x - hi.astype(F32)).astype(BF)


def kernel(cfg, *refs):
    heads, width, tokens, seq_count = cfg
    rows = heads * width
    leaves = tokens // LEAF
    depth_local = leaves.bit_length() - 1
    depth_all = (leaves * seq_count).bit_length() - 1
    levels = list(range(1, depth_all))
    far_levels = [l for l in levels if l >= depth_local]
    scale = math.log2(math.e) / math.sqrt(width)
    refs = list(refs)
    take = lambda n: [refs.pop(0) for _ in range(n)]
    q_hbm, k_hbm, v_hbm, order_hbm, counts_hbm, out = take(6)
    order, counts = take(2)
    xin, xp, kva, ktx, vx, num, stat = take(7)
    us = dict(zip(levels, take(len(levels))))
    qb, kmb, vvb, biasb, fb = take(5)
    fs = dict(zip(far_levels, take(len(far_levels))))
    qs = dict(zip(far_levels, take(len(far_levels))))
    kmp = dict(zip(far_levels, take(len(far_levels))))
    vvp = dict(zip(far_levels, take(len(far_levels))))
    kmr = dict(zip(far_levels, take(len(far_levels))))
    vvr = dict(zip(far_levels, take(len(far_levels))))
    in_sem, halo_send, halo_recv = take(3)
    far_send = dict(zip(far_levels, take(len(far_levels))))
    far_recv = dict(zip(far_levels, take(len(far_levels))))

    seq = lax.axis_index("seq")
    has_left, has_right = seq > 0, seq < seq_count - 1

    loads = [
        pltpu.make_async_copy(src, xin.at[pl.ds(i * rows, rows)], in_sem.at[i])
        for i, src in enumerate((q_hbm, k_hbm, v_hbm))
    ]
    loads.append(pltpu.make_async_copy(order_hbm, order, in_sem.at[3]))
    loads.append(pltpu.make_async_copy(counts_hbm, counts, in_sem.at[4]))
    for load in loads:
        load.start()
    barrier = pltpu.get_barrier_semaphore()
    for step in range(1, seq_count):
        other = lax.rem(seq + step, seq_count)
        pl.semaphore_signal(
            barrier, inc=1, device_id={"seq": other}, device_id_type=pl.DeviceIdType.MESH
        )

    @pl.when(jnp.logical_not(has_left))
    def _():
        ktx[0:LEAF, :] = jnp.zeros((LEAF, rows), BF)
        vx[:, 0:LEAF] = jnp.zeros((rows, LEAF), BF)

    @pl.when(jnp.logical_not(has_right))
    def _():
        ktx[tokens + LEAF :, :] = jnp.zeros((LEAF, rows), BF)
        vx[:, tokens + LEAF :] = jnp.zeros((rows, LEAF), BF)

    def count_of(n):
        leaf = seq * leaves + n
        total = leaves * seq_count
        inside = jnp.logical_and(leaf >= 0, leaf < total)
        return jnp.where(inside, counts[jnp.clip(leaf, 0, total - 1)], 0)

    def build(level):
        u = us[level]
        r = lax.broadcasted_iota(jnp.int32, u.shape, 0)
        t = lax.broadcasted_iota(jnp.int32, u.shape, 1)
        u[...] = jnp.where((t >> level) == r, 1.0, 0.0).astype(BF)

    for level in levels:
        build(level)
    for load in loads:
        load.wait()

    def permute(n):
        at = n * LEAF
        if not isinstance(n, int):
            at = pl.multiple_of(at, LEAF)
        picks = order[0:1, pl.ds(at, LEAF)]
        spots = lax.broadcasted_iota(jnp.int32, (tokens, LEAF), 0)
        hot = jnp.where(spots == picks, 1.0, 0.0).astype(BF)
        moved = dot(xin[...], hot)
        count = count_of(n)
        query, key, value = moved[:rows], moved[rows : 2 * rows], moved[2 * rows :]
        key_t = key.T
        on_row = lax.broadcasted_iota(jnp.int32, (rows, LEAF), 1) < count
        on_col = lax.broadcasted_iota(jnp.int32, (LEAF, rows), 0) < count
        xp[0:rows, pl.ds(at, LEAF)] = query.astype(BF)
        xp[rows : 2 * rows, pl.ds(at, LEAF)] = jnp.where(on_row, value, 0.0).astype(BF)
        xp[2 * rows :, pl.ds(at, LEAF)] = jnp.where(on_row[:PAD], 1.0, 0.0).astype(BF)
        kva[pl.ds(at, LEAF), 0:rows] = jnp.where(on_col, key_t, 0.0).astype(BF)
        kva[pl.ds(at, LEAF), rows:] = jnp.where(on_col, 1.0, 0.0).astype(BF)
        ktx[pl.ds(at + LEAF, LEAF), :] = key_t.astype(BF)
        vx[:, pl.ds(at + LEAF, LEAF)] = value.astype(BF)

    def remote(src, dst, send, recv, target):
        return pltpu.make_async_remote_copy(
            src_ref=src,
            dst_ref=dst,
            send_sem=send,
            recv_sem=recv,
            device_id={"seq": target},
            device_id_type=pl.DeviceIdType.MESH,
        )

    def halo(side):
        start, end = (LEAF, tokens + LEAF) if side == 0 else (tokens, 0)
        target = jnp.maximum(seq - 1, 0) if side == 0 else jnp.minimum(seq + 1, seq_count - 1)
        return (
            remote(
                ktx.at[pl.ds(start, LEAF)],
                ktx.at[pl.ds(end, LEAF)],
                halo_send.at[2 * side],
                halo_recv.at[2 * side],
                target,
            ),
            remote(
                vx.at[:, pl.ds(start, LEAF)],
                vx.at[:, pl.ds(end, LEAF)],
                halo_send.at[2 * side + 1],
                halo_recv.at[2 * side + 1],
                target,
            ),
        )

    @pl.loop(0, leaves)
    def _(i):
        n = jnp.where(i == 0, 0, jnp.where(i == 1, leaves - 1, i - 1))
        permute(n)

        @pl.when(i == 1)
        def _():
            pl.semaphore_wait(barrier, seq_count - 1)

        @pl.when(jnp.logical_and(i == 1, has_left))
        def _():
            for copy in halo(0):
                copy.start()

        @pl.when(jnp.logical_and(i == 1, has_right))
        def _():
            for copy in halo(1):
                copy.start()

    def pool(level, off, span):
        u = us[level][...]
        kk = dot(u, kva[pl.ds(off, span), :])
        mass = kk[:, rows:]
        mean = kk[:, :rows] / jnp.maximum(mass, 1.0)
        xx = dot(xp[:, pl.ds(off, span)], u, ((1,), (1,)))
        q_hi, q_lo = split(xx[:rows] * (1.0 / 2**level))
        return (q_hi, q_lo), mean, xx[rows : 2 * rows], xx[2 * rows :], mass

    def pack(mean, sums, masses):
        v_hi, v_lo = split(sums)
        km = jnp.concatenate(split(mean), axis=1)
        return km, jnp.concatenate([v_hi, v_lo, masses.astype(BF)], axis=0)

    def fixed(x, bound):
        return jnp.floor(x * (STEPS / bound) + 0.5).astype(jnp.int32).astype(jnp.int16)

    def unfixed(x, bound):
        return x.astype(jnp.int32).astype(F32) * (bound / STEPS)

    def only(x, head):
        blank = jnp.zeros((width, x.shape[1]), x.dtype)
        return jnp.concatenate(
            [x[h * width : (h + 1) * width] if h == head else blank for h in range(heads)],
            axis=0,
        )

    def far(query, km, vvs, bias, store):
        q_hi, q_lo = query
        count = q_hi.shape[1]
        for h in range(heads):
            hi, lo = only(q_hi, h), only(q_lo, h)
            s = dot(km, jnp.concatenate([hi, hi], axis=0)) + dot(km[:, :rows], lo)
            if count <= 128:
                s = s + bias[:, :count]
            else:
                s = s + jnp.concatenate([bias[:, :128]] * (count // 128), axis=1)
            best = jnp.max(s, axis=0, keepdims=True).astype(BF)
            w_hi, w_lo = split(jnp.exp2((s - best.astype(F32)) * scale))
            step = 0
            acc = jnp.zeros((width + PAD, count), F32)
            for vv in vvs:
                keys = vv.shape[1]
                v_hi = vv[h * width : (h + 1) * width]
                v_lo = vv[rows + h * width : rows + (h + 1) * width]
                mass = vv[2 * rows :]
                left = jnp.concatenate([v_hi, mass], axis=0)
                both = dot(jnp.concatenate([left, v_lo], axis=0), w_hi[step : step + keys])
                low = jnp.concatenate([both[width + PAD :], jnp.zeros((PAD, count), F32)], axis=0)
                acc = acc + both[: width + PAD] + low + dot(left, w_lo[step : step + keys])
                step += keys
            a_hi, a_lo = split(acc)
            tops = jnp.broadcast_to(best.astype(F32), (PAD, count)).astype(BF)
            store(h, jnp.concatenate([a_hi, a_lo, tops], axis=0))

    def far_copies(level):
        bit = level - depth_local
        nb = 1 << bit
        part = tokens >> level
        slot = lax.rem(seq, nb)
        base = ((seq >> bit) ^ 1) << bit
        copies = []
        for j in range(nb):
            target = base + j
            copies.append(
                remote(
                    kmp[level],
                    kmr[level].at[pl.ds(pl.multiple_of(slot * part, part), part)],
                    far_send[level].at[2 * j],
                    far_recv[level].at[2 * slot],
                    target,
                )
            )
            copies.append(
                remote(
                    vvp[level],
                    vvr[level].at[slot],
                    far_send[level].at[2 * j + 1],
                    far_recv[level].at[2 * slot + 1],
                    target,
                )
            )
        return copies

    for level in reversed(far_levels):
        (q_hi, q_lo), mean, sums, masses, _ = pool(level, 0, tokens)
        qs[level][0:rows, :] = q_hi
        qs[level][rows:, :] = q_lo
        kmp[level][...] = fixed(mean, BOUND)
        vvp[level][0:rows, :] = fixed(sums, BOUND * 2**level)
        vvp[level][rows:, :] = masses.astype(jnp.int32).astype(jnp.int16)
        for copy in far_copies(level):
            copy.start()

    first = 0
    for level in levels:
        if level in far_levels:
            continue
        span = LEAF << level
        blocks = tokens // span
        start = first

        @pl.loop(0, blocks)
        def _(i):
            (q_hi, q_lo), mean, sums, masses, mass = pool(
                level, pl.multiple_of(i * span, span), span
            )
            km, vv = pack(mean, sums, masses)
            qb[start + i, 0:rows, :] = q_hi
            qb[start + i, rows:, :] = q_lo
            kmb[start + i] = km
            vvb[start + i] = vv
            biasb[start + i] = jnp.where(mass > 0, 0.0, NEG)

        first += blocks

    @pl.loop(0, first, unroll=2)
    def _(i):
        query = (qb[i, 0:rows, :], qb[i, rows:, :])
        other = i + 1 - 2 * lax.rem(i, 2)

        def store(h, value):
            fb[i, h] = value

        far(query, kmb[other], [vvb[other]], biasb[other], store)

    def near(n):
        at = n * LEAF
        if not isinstance(n, int):
            at = pl.multiple_of(at, LEAF)
        window = ktx[pl.ds(at, 3 * LEAF), :]
        query = xp[0:rows, pl.ds(at, LEAF)]
        spots = lax.broadcasted_iota(jnp.int32, (LEAF, LEAF), 0)
        for h in range(heads):
            s = dot(window, only(query, h))
            s = jnp.concatenate(
                [
                    jnp.where(spots < count_of(n - 1 + i), s[i * LEAF : (i + 1) * LEAF], NEG)
                    for i in range(3)
                ],
                axis=0,
            )
            best = jnp.max(s, axis=0, keepdims=True)
            w = jnp.exp2((s - best) * scale)
            total = jnp.sum(w, axis=0, keepdims=True)
            value = vx[h * width : (h + 1) * width, pl.ds(at, 3 * LEAF)]
            num[h * width : (h + 1) * width, pl.ds(at, LEAF)] = dot(value, w.astype(BF))
            stat[2 * h : 2 * h + 1, pl.ds(at, LEAF)] = best
            stat[2 * h + 1 : 2 * h + 2, pl.ds(at, LEAF)] = total

    if leaves > 2:

        @pl.loop(1, leaves - 1, unroll=2)
        def _(n):
            near(n)

    @pl.when(has_right)
    def _():
        for copy in halo(0):
            copy.wait_recv()

    @pl.when(has_left)
    def _():
        for copy in halo(1):
            copy.wait_recv()

    @pl.loop(0, 2, unroll=2)
    def _(i):
        near(i * (leaves - 1))

    for level in far_levels:
        nb = 1 << (level - depth_local)
        part = tokens >> level
        for i in range(nb):
            remote(
                kmp[level], kmr[level].at[pl.ds(i * part, part)],
                far_send[level].at[2 * i], far_recv[level].at[2 * i], seq,
            ).wait_recv()
            remote(
                vvp[level], vvr[level].at[i],
                far_send[level].at[2 * i + 1], far_recv[level].at[2 * i + 1], seq,
            ).wait_recv()
        query = (qs[level][0:rows, :], qs[level][rows:, :])
        means = unfixed(kmr[level][...], BOUND)
        vvs = []
        for i in range(nb):
            sums = unfixed(vvr[level][i, 0:rows], BOUND * 2**level)
            masses = vvr[level][i, rows:].astype(jnp.int32).astype(F32)
            km, vv = pack(means, sums, masses)
            vvs.append(vv)
        ones = jnp.ones((PAD, 128), BF)
        mass = jnp.concatenate(
            [dot(vv[2 * rows :], ones, ((0,), (0,))) for vv in vvs], axis=0
        )
        bias = jnp.where(mass > 0, 0.0, NEG)

        def store(h, value):
            fs[level][h] = value

        far(query, km, vvs, bias, store)

    base_of, first = {}, 0
    for level in levels:
        base_of[level] = first
        first += tokens // (LEAF << level)

    def finish(n):
        at = pl.multiple_of(n * LEAF, LEAF)
        for h in range(heads):
            near_best = stat[2 * h : 2 * h + 1, pl.ds(at, LEAF)]
            near_total = stat[2 * h + 1 : 2 * h + 2, pl.ds(at, LEAF)]
            blocks = []
            best = near_best
            size = width + PAD
            for level in levels:
                if level in far_levels:
                    f = fs[level][h]
                    u = us[level][:, pl.ds(at, LEAF)]
                else:
                    g = 1 << level
                    f = fb[base_of[level] + (n >> level), h]
                    u = us[level][:, pl.ds(pl.multiple_of((n & (g - 1)) * LEAF, LEAF), LEAF)]
                up = dot(f, u)
                top = up[2 * size : 2 * size + 1]
                blocks.append((up[:size] + up[size : 2 * size], top))
                best = jnp.maximum(best, top)
            factor = jnp.exp2((near_best - best) * scale)
            top = num[h * width : (h + 1) * width, pl.ds(at, LEAF)] * factor
            bottom = near_total * factor
            for block, level_best in blocks:
                factor = jnp.exp2((level_best - best) * scale)
                top = top + block[:width] * factor
                bottom = bottom + block[width : width + 1] * factor
            out[h * width : (h + 1) * width, pl.ds(at, LEAF)] = (top * (1.0 / bottom)).astype(BF)

    @pl.loop(0, leaves, unroll=2)
    def _(n):
        finish(n)

    @pl.when(has_left)
    def _():
        for copy in halo(0):
            copy.wait_send()

    @pl.when(has_right)
    def _():
        for copy in halo(1):
            copy.wait_send()

    for level in far_levels:
        for copy in far_copies(level):
            copy.wait_send()


def shards(q_heads, k_heads, v_heads, morton_order, leaf_counts):
    heads_real, width, tokens = q_heads.shape
    heads = heads_real + heads_real % 2
    seq_count = lax.axis_size("seq")
    rows = heads * width
    flat = []
    for x in (q_heads, k_heads, v_heads):
        if heads != heads_real:
            x = jnp.concatenate([x, jnp.zeros_like(x[:1])], axis=0)
        flat.append(x.reshape(rows, tokens))
    leaves = tokens // LEAF
    depth_local = leaves.bit_length() - 1
    depth_all = (leaves * seq_count).bit_length() - 1
    levels = list(range(1, depth_all))
    far_levels = [l for l in levels if l >= depth_local]
    coarse = lambda l: min(LEAF, tokens >> l)
    vm = pltpu.VMEM
    scratch = [
        vm(morton_order.shape, jnp.int32),
        pltpu.SMEM(leaf_counts.shape, jnp.int32),
        vm((3 * rows, tokens), BF),
        vm((2 * rows + PAD, tokens), BF),
        vm((tokens, 2 * rows), BF),
        vm((tokens + 2 * LEAF, rows), BF),
        vm((rows, tokens + 2 * LEAF), BF),
        vm((rows, tokens), F32),
        vm((2 * heads + (-2 * heads) % 8, tokens), F32),
    ]
    scratch += [vm((coarse(l), min(LEAF << l, tokens)), BF) for l in levels]
    near_blocks = sum(tokens // (LEAF << l) for l in levels if l not in far_levels)
    scratch += [
        vm((near_blocks, 2 * rows, LEAF), BF),
        vm((near_blocks, LEAF, 2 * rows), BF),
        vm((near_blocks, 2 * rows + PAD, LEAF), BF),
        vm((near_blocks, LEAF, rows), F32),
        vm((near_blocks, heads, 2 * (width + PAD) + PAD, LEAF), BF),
    ]
    scratch += [vm((heads, 2 * (width + PAD) + PAD, tokens >> l), BF) for l in far_levels]
    scratch += [vm((2 * rows, tokens >> l), BF) for l in far_levels]
    scratch += [vm((tokens >> l, rows), jnp.int16) for l in far_levels]
    scratch += [vm((rows + PAD, tokens >> l), jnp.int16) for l in far_levels]
    scratch += [vm((LEAF, rows), jnp.int16) for l in far_levels]
    scratch += [
        vm((1 << (l - depth_local), rows + PAD, tokens >> l), jnp.int16) for l in far_levels
    ]
    sem = pltpu.SemaphoreType.DMA
    scratch += [sem((5,)), sem((4,)), sem((4,))]
    scratch += [sem((2 << (l - depth_local),)) for l in far_levels] * 2
    out = pl.pallas_call(
        functools.partial(kernel, (heads, width, tokens, seq_count)),
        out_shape=jax.ShapeDtypeStruct((rows, tokens), BF),
        in_specs=[pl.BlockSpec(memory_space=pltpu.HBM)] * 5,
        out_specs=pl.BlockSpec(memory_space=pltpu.VMEM),
        scratch_shapes=scratch,
        compiler_params=pltpu.CompilerParams(
            collective_id=0, has_side_effects=True, vmem_limit_bytes=VMEM_LIMIT
        ),
    )(*flat, morton_order, leaf_counts)
    return out.reshape(heads, width, tokens)[:heads_real]


def solution(mesh):
    placed = (
        P("head", None, ("grp", "seq")),
        P("head", None, ("grp", "seq")),
        P("head", None, ("grp", "seq")),
        P(("grp", "seq"), None),
        P("grp"),
    )
    return jax.shard_map(
        shards,
        mesh=mesh,
        in_specs=placed,
        out_specs=P("head", None, ("grp", "seq")),
        check_vma=False,
    )
```

profile of v0, /device:TPU:0, one launch (start us, length us, event | category | flops | bytes accessed | tf_op | source)
XLA Modules:
  0.0 33.2 jit_solution(1598669959911226932)
XLA Ops:
  0.0 31.3 %shard_map.55 = bf16[128,2048]{1,0:T(8,128)(2,1)} custom-call(bf16[128,2048]{1,0:T(8,128)(2,1)} %bitcast.5, bf16[128,2048]{1,0:T(8,128)(2,1)} %bitcast.6, bf16[128,2048]{1,0:T(8,128)(2,1)} %bitcast.7, s32[1,2048]{1,0:T(1,128)} %refs_3_.1, s32[32]{0:T(128)} %refs_4_.1), custom_call_target="tpu_custom_call" | custom-call | tf_op jit(solution)/shard_map/pallas_call | solution.py:473
  31.3 1.9 %copy.7 = bf16[2,64,2048]{2,1,0:T(8,128)(2,1)} copy(bf16[2,64,2048]{2,1,0:T(8,128)(2,1)} %bitcast.4) | data formatting | bytes 1048576
where the time goes:
time: 33.4 us; the launch traced here: 33.2 us
  Pallas kernels  31.3 us (94%)
  local copies, waits for them, and re-layouts  1.88 us (6%)
    pallas_call x1, Pallas kernels, shards(): pl.pallas_call(functools.partial(kernel, (heads, width, tokens, seq_count...  31.3 us
    unnamed x1, local copies, waits for them, and re-layouts  1.88 us

commit v1 on v0

v1 whole, which is shorter than its diff:
```python
import functools
import math

import jax
import jax.numpy as jnp
from jax import lax
from jax.experimental import pallas as pl
from jax.experimental.pallas import tpu as pltpu
from jax.sharding import PartitionSpec as P

LEAF = 256
LANES = 128
NEG = -1e30
BF = jnp.bfloat16
F32 = jnp.float32
I32 = jnp.int32
I16 = jnp.int16
PAD = 16
BOUND = 10.0
STEPS = 32700.0
VMEM_LIMIT = 63 * 1024 * 1024 + 512 * 1024


def dot(a, b, dims=((1,), (0,))):
    return lax.dot_general(a, b, (dims, ((), ())), preferred_element_type=F32)


def split(x):
    hi = x.astype(BF)
    return hi, (x - hi.astype(F32)).astype(BF)


def iota(shape, dim):
    return lax.broadcasted_iota(I32, shape, dim)


def fixed(x, bound):
    return jnp.floor(x * (STEPS / bound) + 0.5).astype(I32).astype(I16)


def unfixed(x, bound):
    return x.astype(I32).astype(F32) * (bound / STEPS)


def plan(tokens, seq_count):
    leaves = tokens // LEAF
    depth_local = leaves.bit_length() - 1
    depth_all = (leaves * seq_count).bit_length() - 1
    levels = list(range(1, depth_all))
    near_levels = [l for l in levels if l < depth_local]
    far_levels = [l for l in levels if l >= depth_local]
    return leaves, depth_local, near_levels, far_levels


def padded(tokens, level):
    return max(LANES, tokens >> level)


def kernel(cfg, *refs):
    heads, width, tokens, seq_count = cfg
    rows = heads * width
    leaves, depth_local, near_levels, far_levels = plan(tokens, seq_count)
    pairs = leaves // 2
    scale = math.log2(math.e) / math.sqrt(width)
    size = width + PAD
    refs = list(refs)
    take = lambda n: [refs.pop(0) for _ in range(n)]
    q_hbm, k_hbm, v_hbm, order_hbm, counts_hbm, out = take(6)
    order, counts = take(2)
    xin, ka, kb, vx, qx, xp, kv = take(7)
    w1, w3, ua, uu = take(4)
    qf, kmf, vvf, fo, fb = take(5)
    pf = take(1)[0]
    ss, sb, num, stat, zb = take(5)
    per_far = lambda: dict(zip(far_levels, take(len(far_levels))))
    kf, qr, kmr2, vvr2, for_, fbr = (per_far() for _ in range(6))
    kmp, vvp, kmr, vvr = (per_far() for _ in range(4))
    in_sem, halo_send, halo_recv = take(3)
    far_send, far_recv = per_far(), per_far()
    us = dict(zip([l for l in far_levels if (LEAF >> l) < 8], refs))

    seq = lax.axis_index("seq")
    has_left, has_right = seq > 0, seq < seq_count - 1

    loads = [
        pltpu.make_async_copy(src, xin.at[pl.ds(i * rows, rows)], in_sem.at[i])
        for i, src in enumerate((q_hbm, k_hbm, v_hbm))
    ]
    loads.append(pltpu.make_async_copy(order_hbm, order, in_sem.at[3]))
    loads.append(pltpu.make_async_copy(counts_hbm, counts, in_sem.at[4]))
    for load in loads:
        load.start()
    barrier = pltpu.get_barrier_semaphore()
    for step in range(1, seq_count):
        other = lax.rem(seq + step, seq_count)
        pl.semaphore_signal(
            barrier, inc=1, device_id={"seq": other}, device_id_type=pl.DeviceIdType.MESH
        )

    @pl.when(jnp.logical_not(has_left))
    def _():
        ka[0:LEAF, :] = jnp.zeros((LEAF, rows), BF)
        vx[:, 0:LEAF] = jnp.zeros((rows, LEAF), BF)

    @pl.when(jnp.logical_not(has_right))
    def _():
        ka[tokens + LEAF :, :] = jnp.zeros((LEAF, rows), BF)
        vx[:, tokens + LEAF :] = jnp.zeros((rows, LEAF), BF)

    def count_of(n):
        leaf = seq * leaves + n
        total = leaves * seq_count
        inside = jnp.logical_and(leaf >= 0, leaf < total)
        return jnp.where(inside, counts[jnp.clip(leaf, 0, total - 1)], 0)

    def ones_where(mask):
        return jnp.where(mask, 1.0, 0.0).astype(BF)

    t = iota((LEAF, LEAF), 0)
    c = iota((LEAF, LEAF), 1)
    for p in range(2):
        w1[p] = ones_where(
            jnp.logical_or(
                jnp.logical_and(c < LANES, (t >> 1) == c),
                jnp.logical_and(c >= LANES, (t >> 2) + 64 * p == c - LANES),
            )
        )
    uu[...] = ones_where((c >> 1) == (t & (LANES - 1)))
    for i, level in enumerate(far_levels):
        t2 = iota((2 * LEAF, LANES), 0)
        c2 = iota((2 * LEAF, LANES), 1)
        for m in range(pairs):
            w3[m, :, i * LANES : (i + 1) * LANES] = ones_where(
                ((t2 + 2 * LEAF * m) >> level) & (LANES - 1) == c2
            )
    ua_levels, ua_at, at = [l for l in near_levels + far_levels if (LEAF >> l) >= 8], {}, 0
    for level in ua_levels:
        n = LEAF >> level
        ua_at[level] = at
        if n % 16 == 0:
            ua[at : at + n, :] = ones_where((iota((n, LEAF), 1) >> level) == iota((n, LEAF), 0))
        else:
            ua[at : at + 16, :] = ones_where((iota((16, LEAF), 1) >> level) == iota((16, LEAF), 0))
        at += max(n, 16)
    for level, u in us.items():
        u[...] = ones_where((iota(u.shape, 1) >> level) == iota(u.shape, 0))

    def tail_rows(cols):
        r = iota((64, cols), 0)
        return ones_where(r == 0)

    for h in range(heads):
        off = (1 - h) * width
        qx[h, off : off + width, :] = jnp.zeros((width, tokens), BF)
        qx[h, 3 * width :, :] = tail_rows(tokens)
        for i in range(qf.shape[0]):
            qf[i, h, 3 * width :, :] = tail_rows(LEAF)
        for level in far_levels:
            qr[level][h, 3 * width :, :] = tail_rows(qr[level].shape[2])

    for load in loads:
        load.wait()

    lane_lo = iota((LEAF, LANES), 1) < width
    lane_is = iota((LEAF, LANES), 1) == width

    def key_tail(key_t, bias):
        shape = key_t.shape
        lo = iota(shape, 1) < width
        at = iota(shape, 1) == width
        rest = jnp.where(at, bias, 0.0)
        rolled = pltpu.roll(key_t, width, 1)
        return jnp.where(lo, key_t, rest), jnp.where(lo, rolled, rest), rolled

    def leaf_bias(count):
        return jnp.where(iota((LEAF, LANES), 0) < count, 0.0, NEG)

    def permute(m):
        for p in range(2):
            n = 2 * m + p
            at = pl.multiple_of(n * LEAF, LEAF)
            picks = order[0:1, pl.ds(at, LEAF)]
            spots = iota((tokens, LEAF), 0)
            hot = jnp.where(spots == picks, 1.0, 0.0).astype(BF)
            moved = dot(xin[...], hot)
            count = count_of(n)
            query, key, value = moved[:rows], moved[rows : 2 * rows], moved[2 * rows :]
            key_t = key.T
            on_row = iota((rows, LEAF), 1) < count
            on_col = iota((LEAF, rows), 0) < count
            tail0, tail1, rolled = key_tail(key_t, leaf_bias(count))
            ka[pl.ds(at + LEAF, LEAF), :] = key_t.astype(BF)
            kb[0, pl.ds(at + LEAF, LEAF), :] = tail0.astype(BF)
            kb[1, pl.ds(at + LEAF, LEAF), :] = tail1.astype(BF)
            kv[pl.ds(at, LEAF), 0:rows] = jnp.where(on_col, key_t, 0.0).astype(BF)
            kv[pl.ds(at, LEAF), rows:] = jnp.where(on_col, rolled, 0.0).astype(BF)
            vx[:, pl.ds(at + LEAF, LEAF)] = value.astype(BF)
            xp[0:rows, pl.ds(at, LEAF)] = query.astype(BF)
            xp[rows : 2 * rows, pl.ds(at, LEAF)] = jnp.where(on_row, value, 0.0).astype(BF)
            xp[2 * rows :, pl.ds(at, LEAF)] = ones_where(on_row[:PAD])
            hi, lo = split(query * scale)
            for h in range(heads):
                part = slice(h * width, (h + 1) * width)
                qx[h, part, pl.ds(at, LEAF)] = hi[part]
                qx[h, 2 * width : 3 * width, pl.ds(at, LEAF)] = lo[part]

    def put_query(ref, x, factor, where):
        hi, lo = split(x * factor)
        for h in range(heads):
            part = slice(h * width, (h + 1) * width)
            ref[h, 0:width, where] = hi[part]
            ref[h, width : 2 * width, where] = hi[part]
            ref[h, 2 * width : 3 * width, where] = lo[part]

    def put_value(ref, x, mass, where):
        hi, lo = split(x)
        for h in range(heads):
            part = slice(h * width, (h + 1) * width)
            ref[h, 0:width, where] = hi[part]
            ref[h, width:size, where] = mass.astype(BF)
            ref[h, size:, where] = lo[part]

    def put_key(ref, a, b, bias, where):
        lo_lane = iota(a.shape, 1) < width
        bias_lane = iota(a.shape, 1) == width
        a_hi, b_hi = a.astype(BF).astype(F32), b.astype(BF).astype(F32)
        rest = jnp.where(bias_lane, bias, 0.0)
        ref[0, where, 0:rows] = jnp.where(lo_lane, a_hi, b - b_hi).astype(BF)
        ref[0, where, rows:] = jnp.where(lo_lane, a_hi, rest).astype(BF)
        ref[1, where, 0:rows] = jnp.where(lo_lane, b_hi, a - a_hi).astype(BF)
        ref[1, where, rows:] = jnp.where(lo_lane, b_hi, rest).astype(BF)

    def clip_mass(count, at, g):
        return jnp.clip(count - at, 0, g).astype(F32)

    base_of, first = {}, 0
    for level in near_levels:
        base_of[level] = first
        first += leaves >> level

    def pool(m):
        start = pl.multiple_of(m * 2 * LEAF, 2 * LEAF)
        t1, kk = [], []
        for p in range(2):
            at = pl.multiple_of(start + p * LEAF, LEAF)
            t1.append(dot(xp[0 : 2 * rows, pl.ds(at, LEAF)], w1[p]))
            kk.append(dot(ua[...], kv[pl.ds(at, LEAF), :]))
        if far_levels:
            pf[m] = dot(xp[:, pl.ds(start, 2 * LEAF)], w3[m])
        n = [count_of(2 * m), count_of(2 * m + 1)]
        b1 = base_of[1] + m
        lane = iota((PAD, LANES), 1)
        for p in range(2):
            where = slice(p * LANES, (p + 1) * LANES)
            put_query(qf.at[b1], t1[p][:rows, :LANES], scale / 2, where)
            put_value(vvf.at[b1], t1[p][rows:, :LANES], clip_mass(n[p], lane << 1, 2), where)
        if 2 in near_levels:
            b2 = base_of[2] + m // 2
            x2 = t1[0][:, LANES:] + t1[1][:, LANES:]
            where = pl.ds(pl.multiple_of((m % 2) * LANES, LANES), LANES)
            mass = jnp.where(
                lane < 64, clip_mass(n[0], lane << 2, 4), clip_mass(n[1], (lane - 64) << 2, 4)
            )
            put_query(qf.at[b2], x2[:rows], scale / 4, where)
            put_value(vvf.at[b2], x2[rows:], mass, where)
        for p in range(2):
            for level in ua_levels:
                count = LEAF >> level
                x = kk[p][ua_at[level] : ua_at[level] + count]
                mass = clip_mass(n[p], iota((count, LANES), 0) << level, 1 << level)
                inverse = 1.0 / jnp.maximum(mass, 1.0)
                a = x[:, :rows] * inverse
                if level in near_levels:
                    b = x[:, rows:] * inverse
                    bias = jnp.where(mass > 0, 0.0, NEG)
                    if level == 1:
                        put_key(kmf.at[b1], a, b, bias, slice(p * count, (p + 1) * count))
                    else:
                        spot = pl.multiple_of((m % 2) * LANES + p * count, count)
                        put_key(kmf.at[b2], a, b, bias, pl.ds(spot, count))
                else:
                    spot = pl.multiple_of((2 * m + p) * count, count)
                    kf[level][pl.ds(spot, count), :] = a

    def remote(src, dst, send, recv, target):
        return pltpu.make_async_remote_copy(
            src_ref=src,
            dst_ref=dst,
            send_sem=send,
            recv_sem=recv,
            device_id={"seq": target},
            device_id_type=pl.DeviceIdType.MESH,
        )

    def halo(side):
        start, end = (LEAF, tokens + LEAF) if side == 0 else (tokens, 0)
        target = jnp.maximum(seq - 1, 0) if side == 0 else jnp.minimum(seq + 1, seq_count - 1)
        return (
            remote(
                ka.at[pl.ds(start, LEAF)],
                ka.at[pl.ds(end, LEAF)],
                halo_send.at[2 * side],
                halo_recv.at[2 * side],
                target,
            ),
            remote(
                vx.at[:, pl.ds(start, LEAF)],
                vx.at[:, pl.ds(end, LEAF)],
                halo_send.at[2 * side + 1],
                halo_recv.at[2 * side + 1],
                target,
            ),
        )

    def pair_at(i):
        return jnp.where(i == 0, 0, jnp.where(i == 1, pairs - 1, i - 1))

    permute(0)

    @pl.loop(1, pairs)
    def _(i):
        pool(pair_at(i - 1))
        permute(pair_at(i))

        @pl.when(i == 1)
        def _():
            pl.semaphore_wait(barrier, seq_count - 1)

        @pl.when(jnp.logical_and(i == 1, has_left))
        def _():
            for copy in halo(0):
                copy.start()

        @pl.when(jnp.logical_and(i == 1, has_right))
        def _():
            for copy in halo(1):
                copy.start()

    pool(pair_at(pairs - 1))

    def far_copies(level):
        bit = level - depth_local
        nb = 1 << bit
        part = tokens >> level
        slot = lax.rem(seq, nb)
        base = ((seq >> bit) ^ 1) << bit
        copies = []
        for j in range(nb):
            target = base + j
            copies.append(
                remote(
                    kmp[level],
                    kmr[level].at[pl.ds(pl.multiple_of(slot * part, part), part)],
                    far_send[level].at[2 * j],
                    far_recv[level].at[2 * slot],
                    target,
                )
            )
            copies.append(
                remote(
                    vvp[level],
                    vvr[level].at[slot],
                    far_send[level].at[2 * j + 1],
                    far_recv[level].at[2 * slot + 1],
                    target,
                )
            )
        return copies

    for i, level in enumerate(far_levels):
        part = tokens >> level
        pieces = part // LANES
        per = pairs // max(pieces, 1)
        cols = slice(i * LANES, (i + 1) * LANES)
        for j in range(max(pieces, 1)):
            x = sum(pf[j * per + e, :, cols] for e in range(per))
            where = slice(j * LANES, (j + 1) * LANES)
            put_query(qr[level], x[:rows], scale / 2**level, where)
            kept = min(LANES, part)
            where = slice(j * kept, (j + 1) * kept)
            vvp[level][0:rows, where] = fixed(x[rows : 2 * rows, :kept], BOUND * 2**level)
            vvp[level][rows:, where] = x[2 * rows :, :kept].astype(I32).astype(I16)
        if level in us:
            sums = dot(us[level][...], kv[:, 0:rows])
            valid = jnp.broadcast_to(xp[2 * rows : 2 * rows + 1, :], (LANES, tokens))
            mass = dot(us[level][...], valid, ((1,), (1,)))
            mean = sums / jnp.maximum(mass, 1.0)
        else:
            mean = kf[level][...]
        kmp[level][...] = fixed(mean, BOUND)
        for copy in far_copies(level):
            copy.start()

    def far_score(km, q, slot, h, best_ref):
        s = dot(km, q)
        keys, cols = s.shape
        ss[slot, h, 0:keys, 0:cols] = s
        best = jnp.max(s.reshape(keys // 8, 8, cols), axis=0)
        best = jnp.max(best, axis=0, keepdims=True).astype(BF).astype(F32)
        best_ref[h] = jnp.broadcast_to(best, (8, cols))

    def far_soft(vvs, slot, h, best_ref, out_ref):
        cols = best_ref.shape[2]
        best = best_ref[h]
        step, acc = 0, None
        for vv in vvs:
            keys = vv.shape[1]
            x = ss[slot, h, step : step + keys, 0:cols].reshape(keys // 8, 8, cols)
            w = jnp.exp2(x - best[None]).reshape(keys, cols)
            w_hi, w_lo = split(w)
            both = dot(vv, w_hi)
            low = jnp.concatenate([both[size:], jnp.zeros((PAD, cols), F32)], axis=0)
            term = both[:size] + low + dot(vv[:size], w_lo)
            acc = term if acc is None else acc + term
            step += keys
        out_ref[h] = acc

    def local_score(i, slot, h):
        far_score(kmf[i ^ 1, h], qf[i, h], slot, h, fb.at[i])

    def local_soft(i, slot, h):
        far_soft([vvf[i ^ 1, h]], slot, h, fb.at[i], fo.at[i])

    for h in range(heads):
        local_score(0, 0, h)

    @pl.loop(0, first // 2)
    def _(b):
        for j in range(2):
            i = 2 * b + j
            for h in range(heads):
                local_soft(i, j, h)
                local_score(jnp.minimum(i + 1, first - 1), 1 - j, h)

    @pl.when(has_right)
    def _():
        for copy in halo(0):
            copy.wait_recv()

    @pl.when(has_left)
    def _():
        for copy in halo(1):
            copy.wait_recv()

    for n, at in ((-1, 0), (leaves, tokens + LEAF)):
        tail0, tail1, _ = key_tail(ka[at : at + LEAF, :].astype(F32), leaf_bias(count_of(n)))
        kb[0, at : at + LEAF, :] = tail0.astype(BF)
        kb[1, at : at + LEAF, :] = tail1.astype(BF)

    def near_score(n, slot, h):
        at = pl.multiple_of(n * LEAF, LEAF)
        best = None
        for j in range(3):
            key_rows = pl.ds(pl.multiple_of(at + j * LEAF, LEAF), LEAF)
            left = jnp.concatenate([ka[key_rows, :], kb[h, key_rows, :]], axis=1)
            s = dot(left, qx[h, :, pl.ds(at, LEAF)])
            ss[slot, h, j * LEAF : (j + 1) * LEAF, :] = s
            top = jnp.max(s.reshape(LEAF // 8, 8, LEAF), axis=0)
            best = top if best is None else jnp.maximum(best, top)
        sb[slot, h] = jnp.broadcast_to(jnp.max(best, axis=0, keepdims=True), (8, LEAF))

    def near_soft(n, slot, h):
        at = pl.multiple_of(n * LEAF, LEAF)
        best = sb[slot, h]
        total, acc = None, None
        part = slice(h * width, (h + 1) * width)
        for j in range(3):
            x = ss[slot, h, j * LEAF : (j + 1) * LEAF, :].reshape(LEAF // 8, 8, LEAF)
            w = jnp.exp2(x - best[None])
            term = jnp.sum(w, axis=0)
            total = term if total is None else total + term
            keys = pl.ds(pl.multiple_of(at + j * LEAF, LEAF), LEAF)
            term = dot(vx[part, keys], w.reshape(LEAF, LEAF).astype(BF))
            acc = term if acc is None else acc + term
        num[part, pl.ds(at, LEAF)] = acc
        stat[2 * h : 2 * h + 1, pl.ds(at, LEAF)] = best[0:1]
        stat[2 * h + 1 : 2 * h + 2, pl.ds(at, LEAF)] = jnp.sum(total, axis=0, keepdims=True)

    for h in range(heads):
        near_score(0, 0, h)

    @pl.loop(0, leaves // 4)
    def _(i):
        for j in range(4):
            n = 4 * i + j
            for h in range(heads):
                near_soft(n, j % 2, h)
                near_score(jnp.minimum(n + 1, leaves - 1), 1 - j % 2, h)

    for slot, level in enumerate(far_levels):
        nb = 1 << (level - depth_local)
        part = tokens >> level
        for i in range(nb):
            remote(
                kmp[level], kmr[level].at[pl.ds(i * part, part)],
                far_send[level].at[2 * i], far_recv[level].at[2 * i], seq,
            ).wait_recv()
            remote(
                vvp[level], vvr[level].at[i],
                far_send[level].at[2 * i + 1], far_recv[level].at[2 * i + 1], seq,
            ).wait_recv()
        ones = jnp.ones((PAD, LANES), BF)
        masses = []
        for i in range(nb):
            mass = vvr[level][i, rows:].astype(I32).astype(F32)
            masses.append(dot(mass.astype(BF), ones, ((0,), (0,))))
            put_value(vvr2[level].at[i], unfixed(vvr[level][i, 0:rows], BOUND * 2**level), mass, slice(0, part))
        bias = jnp.where(jnp.concatenate(masses, axis=0) > 0, 0.0, NEG)
        mean = unfixed(kmr[level][...], BOUND)
        put_key(kmr2[level], mean, pltpu.roll(mean, width, 1), bias, slice(0, LEAF))
        for h in range(heads):
            far_score(kmr2[level][h], qr[level][h], slot % 2, h, fbr[level])
        for h in range(heads):
            far_soft([vvr2[level][i, h] for i in range(nb)], slot % 2, h, fbr[level], for_[level])

    def up(z):
        return dot(jnp.concatenate(split(z), axis=1), uu[...])

    def with_best(acc, best):
        return jnp.concatenate([acc[: size - 8], jnp.broadcast_to(best, (8, acc.shape[1]))], axis=0)

    def merge(acc, best, z):
        old = z[size - 8 : size - 7]
        new = jnp.maximum(best, old)
        both = acc * jnp.exp2(best - new) + z * jnp.exp2(old - new)
        return with_best(both, new)

    for h in range(heads):
        z = None
        for level in reversed(far_levels):
            acc, best = for_[level][h], fbr[level][h, 0:1]
            if z is None:
                z = with_best(acc, best)
            else:
                z = jnp.concatenate(
                    [up(z[:, j * LANES : (j + 1) * LANES]) for j in range(z.shape[1] // LANES)], axis=1
                )[:, : acc.shape[1]]
                z = merge(acc, best, z)
        if z is not None:
            for j in range(z.shape[1] // LANES):
                zb[h, j] = z[:, j * LANES : (j + 1) * LANES]
        for level in reversed(near_levels):
            for i in reversed(range(leaves >> level)):
                block = base_of[level] + i
                acc, best = fo[block, h], fb[block, h, 0:1]
                if z is None:
                    x = with_best(acc, best)
                else:
                    x = merge(acc, best, up(zb[h, i]))
                zb[h, 2 * i] = x[:, :LANES]
                zb[h, 2 * i + 1] = x[:, LANES:]
            z = True
        for n in range(leaves):
            cols = slice(n * LEAF, (n + 1) * LEAF)
            part = slice(h * width, (h + 1) * width)
            near_best, near_total = stat[2 * h : 2 * h + 1, cols], stat[2 * h + 1 : 2 * h + 2, cols]
            z = up(zb[h, n])
            old = z[size - 8 : size - 7]
            new = jnp.maximum(near_best, old)
            mine, other = jnp.exp2(near_best - new), jnp.exp2(old - new)
            inverse = 1.0 / (near_total * mine + z[width : width + 1] * other)
            out[part, cols] = (num[part, cols] * (mine * inverse) + z[:width] * (other * inverse)).astype(BF)

    @pl.when(has_left)
    def _():
        for copy in halo(0):
            copy.wait_send()

    @pl.when(has_right)
    def _():
        for copy in halo(1):
            copy.wait_send()

    for level in far_levels:
        for copy in far_copies(level):
            copy.wait_send()


def shards(q_heads, k_heads, v_heads, morton_order, leaf_counts):
    heads_real, width, tokens = q_heads.shape
    heads = heads_real + heads_real % 2
    seq_count = lax.axis_size("seq")
    rows = heads * width
    flat = []
    for x in (q_heads, k_heads, v_heads):
        if heads != heads_real:
            x = jnp.concatenate([x, jnp.zeros_like(x[:1])], axis=0)
        flat.append(x.reshape(rows, tokens))
    leaves, depth_local, near_levels, far_levels = plan(tokens, seq_count)
    size = width + PAD
    near_blocks = sum(leaves >> l for l in near_levels)
    ua_rows = sum(max(LEAF >> l, 16) for l in near_levels + far_levels if (LEAF >> l) >= 8)
    vm = pltpu.VMEM
    scratch = [
        vm(morton_order.shape, I32),
        pltpu.SMEM(leaf_counts.shape, I32),
        vm((3 * rows, tokens), BF),
        vm((tokens + 2 * LEAF, rows), BF),
        vm((heads, tokens + 2 * LEAF, LANES), BF),
        vm((rows, tokens + 2 * LEAF), BF),
        vm((heads, 4 * width, tokens), BF),
        vm((2 * rows + PAD, tokens), BF),
        vm((tokens, 2 * rows), BF),
        vm((2, LEAF, LEAF), BF),
        vm((leaves // 2, 2 * LEAF, LANES * len(far_levels)), BF),
        vm((ua_rows, LEAF), BF),
        vm((LEAF, LEAF), BF),
        vm((near_blocks, heads, 4 * width, LEAF), BF),
        vm((near_blocks, heads, LEAF, 2 * rows), BF),
        vm((near_blocks, heads, size + width, LEAF), BF),
        vm((near_blocks, heads, size, LEAF), F32),
        vm((near_blocks, heads, 8, LEAF), F32),
        vm((leaves // 2, 2 * rows + PAD, LANES * len(far_levels)), F32),
        vm((2, heads, 3 * LEAF, LEAF), F32),
        vm((2, heads, 8, LEAF), F32),
        vm((rows, tokens), F32),
        vm((2 * heads + (-2 * heads) % 8, tokens), F32),
        vm((heads, leaves, size, LANES), F32),
    ]
    scratch += [vm((tokens >> l, rows), F32) for l in far_levels]
    scratch += [vm((heads, 4 * width, padded(tokens, l)), BF) for l in far_levels]
    scratch += [vm((heads, LEAF, 2 * rows), BF) for l in far_levels]
    scratch += [vm((1 << (l - depth_local), heads, size + width, tokens >> l), BF) for l in far_levels]
    scratch += [vm((heads, size, padded(tokens, l)), F32) for l in far_levels]
    scratch += [vm((heads, 8, padded(tokens, l)), F32) for l in far_levels]
    scratch += [vm((tokens >> l, rows), I16) for l in far_levels]
    scratch += [vm((rows + PAD, tokens >> l), I16) for l in far_levels]
    scratch += [vm((LEAF, rows), I16) for l in far_levels]
    scratch += [vm((1 << (l - depth_local), rows + PAD, tokens >> l), I16) for l in far_levels]
    sem = pltpu.SemaphoreType.DMA
    scratch += [sem((5,)), sem((4,)), sem((4,))]
    scratch += [sem((2 << (l - depth_local),)) for l in far_levels] * 2
    scratch += [vm((tokens >> l, tokens), BF) for l in far_levels if (LEAF >> l) < 8]
    out = pl.pallas_call(
        functools.partial(kernel, (heads, width, tokens, seq_count)),
        out_shape=jax.ShapeDtypeStruct((rows, tokens), BF),
        in_specs=[pl.BlockSpec(memory_space=pltpu.HBM)] * 5,
        out_specs=pl.BlockSpec(memory_space=pltpu.VMEM),
        scratch_shapes=scratch,
        compiler_params=pltpu.CompilerParams(
            collective_id=0, has_side_effects=True, vmem_limit_bytes=VMEM_LIMIT
        ),
    )(*flat, morton_order, leaf_counts)
    return out.reshape(heads, width, tokens)[:heads_real]


def solution(mesh):
    placed = (
        P("head", None, ("grp", "seq")),
        P("head", None, ("grp", "seq")),
        P("head", None, ("grp", "seq")),
        P(("grp", "seq"), None),
        P("grp"),
    )
    return jax.shard_map(
        shards,
        mesh=mesh,
        in_specs=placed,
        out_specs=P("head", None, ("grp", "seq")),
        check_vma=False,
    )
```

time: 33.4 us -> 24.6 us (0.74)
  Pallas kernels: 31.3 us -> 22.6 us
    pallas_call x1, Pallas kernels: 31.3 us -> 22.6 us  [shards(): pl.pallas_call(functools.partial(kernel, (heads, width, tokens, seq_count...]
where the time goes in v1:
time: 24.6 us; the launch traced here: 24.5 us
  Pallas kernels  22.6 us (92%)
  local copies, waits for them, and re-layouts  1.88 us (8%)
    pallas_call x1, Pallas kernels, shards(): pl.pallas_call(functools.partial(kernel, (heads, width, tokens, seq_count...  22.6 us
    unnamed x1, local copies, waits for them, and re-layouts  1.88 us

profile of v1, /device:TPU:0, one launch (start us, length us, event | category | flops | bytes accessed | tf_op | source)
XLA Modules:
  0.0 24.5 jit_solution(3231785256531957567)
XLA Ops:
  0.0 22.6 %shard_map.55 = bf16[128,2048]{1,0:T(8,128)(2,1)} custom-call(bf16[128,2048]{1,0:T(8,128)(2,1)} %bitcast.5, bf16[128,2048]{1,0:T(8,128)(2,1)} %bitcast.6, bf16[128,2048]{1,0:T(8,128)(2,1)} %bitcast.7, s32[1,2048]{1,0:T(1,128)} %refs_3_.1, s32[32]{0:T(128)} %refs_4_.1), custom_call_target="tpu_custom_call" | custom-call | tf_op jit(solution)/shard_map/pallas_call | solution.py:634
  22.6 1.9 %copy.7 = bf16[2,64,2048]{2,1,0:T(8,128)(2,1)} copy(bf16[2,64,2048]{2,1,0:T(8,128)(2,1)} %bitcast.4) | data formatting | bytes 1048576

commit v2 on v1

--- a/solution.py
+++ b/solution.py
@@ -18,7 +18,7 @@
 PAD = 16
 BOUND = 10.0
 STEPS = 32700.0
-VMEM_LIMIT = 63 * 1024 * 1024 + 512 * 1024
+VMEM_LIMIT = 63488 * 1024
 
 
 def dot(a, b, dims=((1,), (0,))):
@@ -633,7 +633,7 @@
     scratch += [vm((tokens >> l, tokens), BF) for l in far_levels if (LEAF >> l) < 8]
     out = pl.pallas_call(
         functools.partial(kernel, (heads, width, tokens, seq_count)),
-        out_shape=jax.ShapeDtypeStruct((rows, tokens), BF),
+        out_shape=pltpu.VMEM((rows, tokens), BF),
         in_specs=[pl.BlockSpec(memory_space=pltpu.HBM)] * 5,
         out_specs=pl.BlockSpec(memory_space=pltpu.VMEM),
         scratch_shapes=scratch,

time: 24.6 us -> 22.7 us (0.923)
  local copies, waits for them, and re-layouts: 1.88 us -> 0.8 us
  Pallas kernels: 22.6 us -> 21.8 us
    unnamed x1, local copies, waits for them, and re-layouts: 1.88 us -> 0.8 us
    pallas_call x1, Pallas kernels: 22.6 us -> 21.8 us  [shards(): pl.pallas_call(functools.partial(kernel, (heads, width, tokens, seq_count...]
where the time goes in v2:
time: 22.7 us; the launch traced here: 22.6 us
  Pallas kernels  21.8 us (96%)
  local copies, waits for them, and re-layouts  0.8 us (4%)
    pallas_call x1, Pallas kernels, shards(): pl.pallas_call(functools.partial(kernel, (heads, width, tokens, seq_count...  21.8 us
    unnamed x1, local copies, waits for them, and re-layouts  0.8 us

profile of v2, /device:TPU:0, one launch (start us, length us, event | category | flops | bytes accessed | tf_op | source)
XLA Modules:
  0.0 22.6 jit_solution(511188923009934593)
XLA Ops:
  0.0 21.8 %shard_map.55 = bf16[128,2048]{1,0:T(8,128)(2,1)S(1)} custom-call(bf16[128,2048]{1,0:T(8,128)(2,1)} %bitcast.5, bf16[128,2048]{1,0:T(8,128)(2,1)} %bitcast.6, bf16[128,2048]{1,0:T(8,128)(2,1)} %bitcast.7, s32[1,2048]{1,0:T(1,128)} %refs_3_.1, s32[32]{0:T(128)} %refs_4_.1), custom_call_target="tpu_custom_call" | custom-call | tf_op jit(solution)/shard_map/pallas_call | solution.py:634
  21.8 0.8 %copy.7 = bf16[2,64,2048]{2,1,0:T(8,128)(2,1)} copy(bf16[2,64,2048]{2,1,0:T(8,128)(2,1)S(1)} %bitcast.4) | data formatting | bytes 1048576

commit v3 on v2

--- a/solution.py
+++ b/solution.py
@@ -68,16 +68,16 @@
     q_hbm, k_hbm, v_hbm, order_hbm, counts_hbm, out = take(6)
     order, counts = take(2)
     xin, ka, kb, vx, qx, xp, kv = take(7)
-    w1, w3, ua, uu = take(4)
+    w1, w3, ua, uf, uu = take(5)
     qf, kmf, vvf, fo, fb = take(5)
     pf = take(1)[0]
     ss, sb, num, stat, zb = take(5)
     per_far = lambda: dict(zip(far_levels, take(len(far_levels))))
-    kf, qr, kmr2, vvr2, for_, fbr = (per_far() for _ in range(6))
-    kmp, vvp, kmr, vvr = (per_far() for _ in range(4))
+    qr, kmr2, vvr2, for_, fbr, fp, fr = (per_far() for _ in range(7))
     in_sem, halo_send, halo_recv = take(3)
     far_send, far_recv = per_far(), per_far()
     us = dict(zip([l for l in far_levels if (LEAF >> l) < 8], refs))
+    pieced = [l for l in far_levels if l not in us]
 
     seq = lax.axis_index("seq")
     has_left, has_right = seq > 0, seq < seq_count - 1
@@ -133,15 +133,14 @@
             w3[m, :, i * LANES : (i + 1) * LANES] = ones_where(
                 ((t2 + 2 * LEAF * m) >> level) & (LANES - 1) == c2
             )
-    ua_levels, ua_at, at = [l for l in near_levels + far_levels if (LEAF >> l) >= 8], {}, 0
-    for level in ua_levels:
-        n = LEAF >> level
-        ua_at[level] = at
-        if n % 16 == 0:
-            ua[at : at + n, :] = ones_where((iota((n, LEAF), 1) >> level) == iota((n, LEAF), 0))
-        else:
-            ua[at : at + 16, :] = ones_where((iota((16, LEAF), 1) >> level) == iota((16, LEAF), 0))
-        at += max(n, 16)
+    ua_at, uf_at = {}, {}
+    for ref, spots, which in ((ua, ua_at, near_levels), (uf, uf_at, pieced)):
+        at = 0
+        for level in which:
+            n = max(LEAF >> level, 16)
+            spots[level] = at
+            ref[at : at + n, :] = ones_where((iota((n, LEAF), 1) >> level) == iota((n, LEAF), 0))
+            at += n
     for level, u in us.items():
         u[...] = ones_where((iota(u.shape, 1) >> level) == iota(u.shape, 0))
 
@@ -192,8 +191,9 @@
             ka[pl.ds(at + LEAF, LEAF), :] = key_t.astype(BF)
             kb[0, pl.ds(at + LEAF, LEAF), :] = tail0.astype(BF)
             kb[1, pl.ds(at + LEAF, LEAF), :] = tail1.astype(BF)
-            kv[pl.ds(at, LEAF), 0:rows] = jnp.where(on_col, key_t, 0.0).astype(BF)
-            kv[pl.ds(at, LEAF), rows:] = jnp.where(on_col, rolled, 0.0).astype(BF)
+            kv[pl.ds(at, LEAF), 0:rows] = jnp.where(on_col, rolled, 0.0).astype(BF)
+            kv[pl.ds(at, LEAF), rows : 2 * rows] = jnp.where(on_col, key_t, 0.0).astype(BF)
+            kv[pl.ds(at, LEAF), 2 * rows :] = jnp.where(on_col, value.T, 0.0).astype(BF)
             vx[:, pl.ds(at + LEAF, LEAF)] = value.astype(BF)
             xp[0:rows, pl.ds(at, LEAF)] = query.astype(BF)
             xp[rows : 2 * rows, pl.ds(at, LEAF)] = jnp.where(on_row, value, 0.0).astype(BF)
@@ -238,15 +238,34 @@
         base_of[level] = first
         first += leaves >> level
 
-    def pool(m):
+    def pool_far(m):
+        if not pieced:
+            return
+        start = pl.multiple_of(m * 2 * LEAF, 2 * LEAF)
+        kk = []
+        for p in range(2):
+            at = pl.multiple_of(start + p * LEAF, LEAF)
+            kk.append(dot(uf[...], kv[pl.ds(at, LEAF), rows:]))
+        for level in pieced:
+            count = LEAF >> level
+            x = jnp.concatenate([k[uf_at[level] : uf_at[level] + count] for k in kk], axis=0)
+            mass = [
+                clip_mass(count_of(2 * m + p), iota((count, LANES), 0) << level, 1 << level)
+                for p in range(2)
+            ]
+            mean = x[:, :rows] / jnp.maximum(jnp.concatenate(mass, axis=0), 1.0)
+            fp[level][m, :, 0:rows] = fixed(mean, BOUND)
+            fp[level][m, :, rows:] = fixed(x[:, rows:], BOUND * 2**level)
+
+    def pool_near(m):
         start = pl.multiple_of(m * 2 * LEAF, 2 * LEAF)
         t1, kk = [], []
         for p in range(2):
             at = pl.multiple_of(start + p * LEAF, LEAF)
             t1.append(dot(xp[0 : 2 * rows, pl.ds(at, LEAF)], w1[p]))
-            kk.append(dot(ua[...], kv[pl.ds(at, LEAF), :]))
+            kk.append(dot(ua[...], kv[pl.ds(at, LEAF), 0 : 2 * rows]))
         if far_levels:
-            pf[m] = dot(xp[:, pl.ds(start, 2 * LEAF)], w3[m])
+            pf[m] = dot(xp[0:rows, pl.ds(start, 2 * LEAF)], w3[m])
         n = [count_of(2 * m), count_of(2 * m + 1)]
         b1 = base_of[1] + m
         lane = iota((PAD, LANES), 1)
@@ -264,23 +283,18 @@
             put_query(qf.at[b2], x2[:rows], scale / 4, where)
             put_value(vvf.at[b2], x2[rows:], mass, where)
         for p in range(2):
-            for level in ua_levels:
+            for level in near_levels:
                 count = LEAF >> level
                 x = kk[p][ua_at[level] : ua_at[level] + count]
                 mass = clip_mass(n[p], iota((count, LANES), 0) << level, 1 << level)
                 inverse = 1.0 / jnp.maximum(mass, 1.0)
-                a = x[:, :rows] * inverse
-                if level in near_levels:
-                    b = x[:, rows:] * inverse
-                    bias = jnp.where(mass > 0, 0.0, NEG)
-                    if level == 1:
-                        put_key(kmf.at[b1], a, b, bias, slice(p * count, (p + 1) * count))
-                    else:
-                        spot = pl.multiple_of((m % 2) * LANES + p * count, count)
-                        put_key(kmf.at[b2], a, b, bias, pl.ds(spot, count))
+                b, a = x[:, :rows] * inverse, x[:, rows:] * inverse
+                bias = jnp.where(mass > 0, 0.0, NEG)
+                if level == 1:
+                    put_key(kmf.at[b1], a, b, bias, slice(p * count, (p + 1) * count))
                 else:
-                    spot = pl.multiple_of((2 * m + p) * count, count)
-                    kf[level][pl.ds(spot, count), :] = a
+                    spot = pl.multiple_of((m % 2) * LANES + p * count, count)
+                    put_key(kmf.at[b2], a, b, bias, pl.ds(spot, count))
 
     def remote(src, dst, send, recv, target):
         return pltpu.make_async_remote_copy(
@@ -315,11 +329,28 @@
     def pair_at(i):
         return jnp.where(i == 0, 0, jnp.where(i == 1, pairs - 1, i - 1))
 
+    def far_copies(level, piece):
+        bit = level - depth_local
+        nb = 1 << bit
+        pieces = fp[level].shape[0]
+        slot = lax.rem(seq, nb)
+        base = ((seq >> bit) ^ 1) << bit
+        return [
+            remote(
+                fp[level].at[piece],
+                fr[level].at[slot, piece],
+                far_send[level].at[j * pieces + piece],
+                far_recv[level].at[slot * pieces + piece],
+                base + j,
+            )
+            for j in range(nb)
+        ]
+
     permute(0)
 
     @pl.loop(1, pairs)
     def _(i):
-        pool(pair_at(i - 1))
+        pool_far(pair_at(i - 1))
         permute(pair_at(i))
 
         @pl.when(i == 1)
@@ -336,60 +367,34 @@
             for copy in halo(1):
                 copy.start()
 
-    pool(pair_at(pairs - 1))
-
-    def far_copies(level):
-        bit = level - depth_local
-        nb = 1 << bit
-        part = tokens >> level
-        slot = lax.rem(seq, nb)
-        base = ((seq >> bit) ^ 1) << bit
-        copies = []
-        for j in range(nb):
-            target = base + j
-            copies.append(
-                remote(
-                    kmp[level],
-                    kmr[level].at[pl.ds(pl.multiple_of(slot * part, part), part)],
-                    far_send[level].at[2 * j],
-                    far_recv[level].at[2 * slot],
-                    target,
-                )
-            )
-            copies.append(
-                remote(
-                    vvp[level],
-                    vvr[level].at[slot],
-                    far_send[level].at[2 * j + 1],
-                    far_recv[level].at[2 * slot + 1],
-                    target,
-                )
-            )
-        return copies
+        for level in reversed(pieced):
+            for copy in far_copies(level, pair_at(i - 1)):
+                copy.start()
+
+    pool_far(pair_at(pairs - 1))
+    for level in reversed(pieced):
+        for copy in far_copies(level, pair_at(pairs - 1)):
+            copy.start()
+    for level in us:
+        sums = dot(us[level][...], kv[:, rows:])
+        valid = jnp.broadcast_to(xp[2 * rows : 2 * rows + 1, :], (LANES, tokens))
+        mass = dot(us[level][...], valid, ((1,), (1,)))
+        fp[level][0, :, 0:rows] = fixed(sums[:, :rows] / jnp.maximum(mass, 1.0), BOUND)
+        fp[level][0, :, rows:] = fixed(sums[:, rows:], BOUND * 2**level)
+        for copy in far_copies(level, 0):
+            copy.start()
+
+    @pl.loop(0, pairs)
+    def _(m):
+        pool_near(m)
 
     for i, level in enumerate(far_levels):
-        part = tokens >> level
-        pieces = part // LANES
-        per = pairs // max(pieces, 1)
+        pieces = max((tokens >> level) // LANES, 1)
+        per = pairs // pieces
         cols = slice(i * LANES, (i + 1) * LANES)
-        for j in range(max(pieces, 1)):
+        for j in range(pieces):
             x = sum(pf[j * per + e, :, cols] for e in range(per))
-            where = slice(j * LANES, (j + 1) * LANES)
-            put_query(qr[level], x[:rows], scale / 2**level, where)
-            kept = min(LANES, part)
-            where = slice(j * kept, (j + 1) * kept)
-            vvp[level][0:rows, where] = fixed(x[rows : 2 * rows, :kept], BOUND * 2**level)
-            vvp[level][rows:, where] = x[2 * rows :, :kept].astype(I32).astype(I16)
-        if level in us:
-            sums = dot(us[level][...], kv[:, 0:rows])
-            valid = jnp.broadcast_to(xp[2 * rows : 2 * rows + 1, :], (LANES, tokens))
-            mass = dot(us[level][...], valid, ((1,), (1,)))
-            mean = sums / jnp.maximum(mass, 1.0)
-        else:
-            mean = kf[level][...]
-        kmp[level][...] = fixed(mean, BOUND)
-        for copy in far_copies(level):
-            copy.start()
+            put_query(qr[level], x, scale / 2**level, slice(j * LANES, (j + 1) * LANES))
 
     def far_score(km, q, slot, h, best_ref):
         s = dot(km, q)
@@ -487,31 +492,36 @@
                 near_soft(n, j % 2, h)
                 near_score(jnp.minimum(n + 1, leaves - 1), 1 - j % 2, h)
 
-    for slot, level in enumerate(far_levels):
-        nb = 1 << (level - depth_local)
+    for slot, level in enumerate(reversed(far_levels)):
+        bit = level - depth_local
+        nb = 1 << bit
         part = tokens >> level
+        pieces = fp[level].shape[0]
+        base = ((seq >> bit) ^ 1) << bit
+        lane = iota((PAD, LEAF), 1)
+        count = jnp.zeros((PAD, LEAF), I32)
+        for leaf in range(leaves * nb):
+            count = jnp.where((lane << level) >> 8 == leaf, counts[base * leaves + leaf], count)
+        mass = clip_mass(count, (lane << level) & (LEAF - 1), 1 << level)
+        mass_col = dot(mass.astype(BF), jnp.ones((PAD, LANES), BF), ((0,), (0,)))
+        bias = jnp.where(mass_col > 0, 0.0, NEG)
         for i in range(nb):
-            remote(
-                kmp[level], kmr[level].at[pl.ds(i * part, part)],
-                far_send[level].at[2 * i], far_recv[level].at[2 * i], seq,
-            ).wait_recv()
-            remote(
-                vvp[level], vvr[level].at[i],
-                far_send[level].at[2 * i + 1], far_recv[level].at[2 * i + 1], seq,
-            ).wait_recv()
-        ones = jnp.ones((PAD, LANES), BF)
-        masses = []
-        for i in range(nb):
-            mass = vvr[level][i, rows:].astype(I32).astype(F32)
-            masses.append(dot(mass.astype(BF), ones, ((0,), (0,))))
-            put_value(vvr2[level].at[i], unfixed(vvr[level][i, 0:rows], BOUND * 2**level), mass, slice(0, part))
-        bias = jnp.where(jnp.concatenate(masses, axis=0) > 0, 0.0, NEG)
-        mean = unfixed(kmr[level][...], BOUND)
+            for piece in range(pieces):
+                remote(
+                    fp[level].at[piece], fr[level].at[i, piece],
+                    far_send[level].at[i * pieces + piece], far_recv[level].at[i * pieces + piece], seq,
+                ).wait_recv()
+        got = jnp.concatenate(
+            [fr[level][i, piece].astype(I32).astype(F32) for i in range(nb) for piece in range(pieces)],
+            axis=0,
+        )
+        mean = got[:, :rows] * (BOUND / STEPS)
         put_key(kmr2[level], mean, pltpu.roll(mean, width, 1), bias, slice(0, LEAF))
+        put_value(vvr2[level], got[:, rows:].T * (BOUND * 2**level / STEPS), mass, slice(0, LEAF))
         for h in range(heads):
             far_score(kmr2[level][h], qr[level][h], slot % 2, h, fbr[level])
         for h in range(heads):
-            far_soft([vvr2[level][i, h] for i in range(nb)], slot % 2, h, fbr[level], for_[level])
+            far_soft([vvr2[level][h]], slot % 2, h, fbr[level], for_[level])
 
     def up(z):
         return dot(jnp.concatenate(split(z), axis=1), uu[...])
@@ -572,8 +582,9 @@
             copy.wait_send()
 
     for level in far_levels:
-        for copy in far_copies(level):
-            copy.wait_send()
+        for piece in range(fp[level].shape[0]):
+            for copy in far_copies(level, piece):
+                copy.wait_send()
 
 
 def shards(q_heads, k_heads, v_heads, morton_order, leaf_counts):
@@ -589,7 +600,9 @@
     leaves, depth_local, near_levels, far_levels = plan(tokens, seq_count)
     size = width + PAD
     near_blocks = sum(leaves >> l for l in near_levels)
-    ua_rows = sum(max(LEAF >> l, 16) for l in near_levels + far_levels if (LEAF >> l) >= 8)
+    pieced = [l for l in far_levels if (LEAF >> l) >= 8]
+    unit_rows = lambda which: max(sum(max(LEAF >> l, 16) for l in which), 16)
+    pieces = lambda l: leaves // 2 if l in pieced else 1
     vm = pltpu.VMEM
     scratch = [
         vm(morton_order.shape, I32),
@@ -600,36 +613,35 @@
         vm((rows, tokens + 2 * LEAF), BF),
         vm((heads, 4 * width, tokens), BF),
         vm((2 * rows + PAD, tokens), BF),
-        vm((tokens, 2 * rows), BF),
+        vm((tokens, 3 * rows), BF),
         vm((2, LEAF, LEAF), BF),
         vm((leaves // 2, 2 * LEAF, LANES * len(far_levels)), BF),
-        vm((ua_rows, LEAF), BF),
+        vm((unit_rows(near_levels), LEAF), BF),
+        vm((unit_rows(pieced), LEAF), BF),
         vm((LEAF, LEAF), BF),
         vm((near_blocks, heads, 4 * width, LEAF), BF),
         vm((near_blocks, heads, LEAF, 2 * rows), BF),
         vm((near_blocks, heads, size + width, LEAF), BF),
         vm((near_blocks, heads, size, LEAF), F32),
         vm((near_blocks, heads, 8, LEAF), F32),
-        vm((leaves // 2, 2 * rows + PAD, LANES * len(far_levels)), F32),
+        vm((leaves // 2, rows, LANES * len(far_levels)), F32),
         vm((2, heads, 3 * LEAF, LEAF), F32),
         vm((2, heads, 8, LEAF), F32),
         vm((rows, tokens), F32),
         vm((2 * heads + (-2 * heads) % 8, tokens), F32),
         vm((heads, leaves, size, LANES), F32),
     ]
-    scratch += [vm((tokens >> l, rows), F32) for l in far_levels]
     scratch += [vm((heads, 4 * width, padded(tokens, l)), BF) for l in far_levels]
     scratch += [vm((heads, LEAF, 2 * rows), BF) for l in far_levels]
-    scratch += [vm((1 << (l - depth_local), heads, size + width, tokens >> l), BF) for l in far_levels]
+    scratch += [vm((heads, size + width, LEAF), BF) for l in far_levels]
     scratch += [vm((heads, size, padded(tokens, l)), F32) for l in far_levels]
     scratch += [vm((heads, 8, padded(tokens, l)), F32) for l in far_levels]
-    scratch += [vm((tokens >> l, rows), I16) for l in far_levels]
-    scratch += [vm((rows + PAD, tokens >> l), I16) for l in far_levels]
-    scratch += [vm((LEAF, rows), I16) for l in far_levels]
-    scratch += [vm((1 << (l - depth_local), rows + PAD, tokens >> l), I16) for l in far_levels]
+    sent = lambda l: (pieces(l), (tokens >> l) // pieces(l), 2 * rows)
+    scratch += [vm(sent(l), I16) for l in far_levels]
+    scratch += [vm((1 << (l - depth_local), *sent(l)), I16) for l in far_levels]
     sem = pltpu.SemaphoreType.DMA
     scratch += [sem((5,)), sem((4,)), sem((4,))]
-    scratch += [sem((2 << (l - depth_local),)) for l in far_levels] * 2
+    scratch += [sem((pieces(l) << (l - depth_local),)) for l in far_levels] * 2
     scratch += [vm((tokens >> l, tokens), BF) for l in far_levels if (LEAF >> l) < 8]
     out = pl.pallas_call(
         functools.partial(kernel, (heads, width, tokens, seq_count)),

time: 22.7 us -> 21.4 us (0.943)
  Pallas kernels: 21.8 us -> 20.4 us
    pallas_call x1, Pallas kernels: 21.8 us -> 20.4 us  [shards(): pl.pallas_call(functools.partial(kernel, (heads, width, tokens, seq_count...]
where the time goes in v3:
time: 21.4 us; the launch traced here: 21.2 us
  Pallas kernels  20.4 us (95%)
  local copies, waits for them, and re-layouts  0.8 us (4%)
    pallas_call x1, Pallas kernels, shards(): pl.pallas_call(functools.partial(kernel, (heads, width, tokens, seq_count...  20.4 us
    unnamed x1, local copies, waits for them, and re-layouts  0.8 us

profile of v3, /device:TPU:0, one launch (start us, length us, event | category | flops | bytes accessed | tf_op | source)
XLA Modules:
  0.0 21.2 jit_solution(15679025467929292761)
XLA Ops:
  0.0 20.4 %shard_map.55 = bf16[128,2048]{1,0:T(8,128)(2,1)S(1)} custom-call(bf16[128,2048]{1,0:T(8,128)(2,1)} %bitcast.5, bf16[128,2048]{1,0:T(8,128)(2,1)} %bitcast.6, bf16[128,2048]{1,0:T(8,128)(2,1)} %bitcast.7, s32[1,2048]{1,0:T(1,128)} %refs_3_.1, s32[32]{0:T(128)} %refs_4_.1), custom_call_target="tpu_custom_call" | custom-call | tf_op jit(solution)/shard_map/pallas_call | solution.py:646
  20.4 0.8 %copy.7 = bf16[2,64,2048]{2,1,0:T(8,128)(2,1)} copy(bf16[2,64,2048]{2,1,0:T(8,128)(2,1)S(1)} %bitcast.4) | data formatting | bytes 1048576

commit v4 on v3

--- a/solution.py
+++ b/solution.py
@@ -384,7 +384,7 @@
         for copy in far_copies(level, 0):
             copy.start()
 
-    @pl.loop(0, pairs)
+    @pl.loop(0, pairs, unroll=2)
     def _(m):
         pool_near(m)
 
@@ -492,11 +492,18 @@
                 near_soft(n, j % 2, h)
                 near_score(jnp.minimum(n + 1, leaves - 1), 1 - j % 2, h)
 
-    for slot, level in enumerate(reversed(far_levels)):
+    for level in reversed(far_levels):
+        pieces = fp[level].shape[0]
+        for i in range(1 << (level - depth_local)):
+            for piece in range(pieces):
+                remote(
+                    fp[level].at[piece], fr[level].at[i, piece],
+                    far_send[level].at[i * pieces + piece], far_recv[level].at[i * pieces + piece], seq,
+                ).wait_recv()
+
+    def unpack(level):
         bit = level - depth_local
         nb = 1 << bit
-        part = tokens >> level
-        pieces = fp[level].shape[0]
         base = ((seq >> bit) ^ 1) << bit
         lane = iota((PAD, LEAF), 1)
         count = jnp.zeros((PAD, LEAF), I32)
@@ -505,23 +512,28 @@
         mass = clip_mass(count, (lane << level) & (LEAF - 1), 1 << level)
         mass_col = dot(mass.astype(BF), jnp.ones((PAD, LANES), BF), ((0,), (0,)))
         bias = jnp.where(mass_col > 0, 0.0, NEG)
-        for i in range(nb):
-            for piece in range(pieces):
-                remote(
-                    fp[level].at[piece], fr[level].at[i, piece],
-                    far_send[level].at[i * pieces + piece], far_recv[level].at[i * pieces + piece], seq,
-                ).wait_recv()
         got = jnp.concatenate(
-            [fr[level][i, piece].astype(I32).astype(F32) for i in range(nb) for piece in range(pieces)],
+            [
+                fr[level][i, piece].astype(I32).astype(F32)
+                for i in range(nb)
+                for piece in range(fp[level].shape[0])
+            ],
             axis=0,
         )
         mean = got[:, :rows] * (BOUND / STEPS)
         put_key(kmr2[level], mean, pltpu.roll(mean, width, 1), bias, slice(0, LEAF))
         put_value(vvr2[level], got[:, rows:].T * (BOUND * 2**level / STEPS), mass, slice(0, LEAF))
-        for h in range(heads):
-            far_score(kmr2[level][h], qr[level][h], slot % 2, h, fbr[level])
-        for h in range(heads):
-            far_soft([vvr2[level][h]], slot % 2, h, fbr[level], for_[level])
+
+    for first_level in range(0, len(far_levels), 2):
+        group = list(reversed(far_levels))[first_level : first_level + 2]
+        for level in group:
+            unpack(level)
+        for slot, level in enumerate(group):
+            for h in range(heads):
+                far_score(kmr2[level][h], qr[level][h], slot, h, fbr[level])
+        for slot, level in enumerate(group):
+            for h in range(heads):
+                far_soft([vvr2[level][h]], slot, h, fbr[level], for_[level])
 
     def up(z):
         return dot(jnp.concatenate(split(z), axis=1), uu[...])
@@ -535,39 +547,39 @@
         both = acc * jnp.exp2(best - new) + z * jnp.exp2(old - new)
         return with_best(both, new)
 
-    for h in range(heads):
-        z = None
-        for level in reversed(far_levels):
+    def tiles(z):
+        return [z[:, j * LANES : (j + 1) * LANES] for j in range(z.shape[1] // LANES)]
+
+    zs = [None] * heads
+    for level in reversed(far_levels):
+        for h in range(heads):
             acc, best = for_[level][h], fbr[level][h, 0:1]
-            if z is None:
-                z = with_best(acc, best)
+            if zs[h] is None:
+                zs[h] = with_best(acc, best)
             else:
-                z = jnp.concatenate(
-                    [up(z[:, j * LANES : (j + 1) * LANES]) for j in range(z.shape[1] // LANES)], axis=1
-                )[:, : acc.shape[1]]
-                z = merge(acc, best, z)
-        if z is not None:
-            for j in range(z.shape[1] // LANES):
-                zb[h, j] = z[:, j * LANES : (j + 1) * LANES]
-        for level in reversed(near_levels):
-            for i in reversed(range(leaves >> level)):
+                z = jnp.concatenate([up(x) for x in tiles(zs[h])], axis=1)
+                zs[h] = merge(acc, best, z[:, : acc.shape[1]])
+    zs = [None if z is None else tiles(z) for z in zs]
+    for level in reversed(near_levels):
+        new = [[] for _ in range(heads)]
+        for i in range(leaves >> level):
+            for h in range(heads):
                 block = base_of[level] + i
                 acc, best = fo[block, h], fb[block, h, 0:1]
-                if z is None:
-                    x = with_best(acc, best)
-                else:
-                    x = merge(acc, best, up(zb[h, i]))
-                zb[h, 2 * i] = x[:, :LANES]
-                zb[h, 2 * i + 1] = x[:, LANES:]
-            z = True
-        for n in range(leaves):
+                x = with_best(acc, best) if zs[h] is None else merge(acc, best, up(zs[h][i]))
+                for j, part in enumerate(tiles(x)):
+                    zb[level % 2, h, 2 * i + j] = part
+                    new[h].append(zb.at[level % 2, h, 2 * i + j])
+        zs = [[ref[...] for ref in refs_h] for refs_h in new]
+    for n in range(leaves):
+        for h in range(heads):
             cols = slice(n * LEAF, (n + 1) * LEAF)
             part = slice(h * width, (h + 1) * width)
             near_best, near_total = stat[2 * h : 2 * h + 1, cols], stat[2 * h + 1 : 2 * h + 2, cols]
-            z = up(zb[h, n])
+            z = up(zs[h][n])
             old = z[size - 8 : size - 7]
-            new = jnp.maximum(near_best, old)
-            mine, other = jnp.exp2(near_best - new), jnp.exp2(old - new)
+            new_best = jnp.maximum(near_best, old)
+            mine, other = jnp.exp2(near_best - new_best), jnp.exp2(old - new_best)
             inverse = 1.0 / (near_total * mine + z[width : width + 1] * other)
             out[part, cols] = (num[part, cols] * (mine * inverse) + z[:width] * (other * inverse)).astype(BF)
 
@@ -629,7 +641,7 @@
         vm((2, heads, 8, LEAF), F32),
         vm((rows, tokens), F32),
         vm((2 * heads + (-2 * heads) % 8, tokens), F32),
-        vm((heads, leaves, size, LANES), F32),
+        vm((2, heads, leaves, size, LANES), F32),
     ]
     scratch += [vm((heads, 4 * width, padded(tokens, l)), BF) for l in far_levels]
     scratch += [vm((heads, LEAF, 2 * rows), BF) for l in far_levels]

time: 21.4 us -> 20.5 us (0.958)
  Pallas kernels: 20.4 us -> 19.6 us
    pallas_call x1, Pallas kernels: 20.4 us -> 19.6 us  [shards(): pl.pallas_call(functools.partial(kernel, (heads, width, tokens, seq_count...]
where the time goes in v4:
time: 20.5 us; the launch traced here: 20.4 us
  Pallas kernels  19.6 us (96%)
  local copies, waits for them, and re-layouts  0.8 us (4%)
    pallas_call x1, Pallas kernels, shards(): pl.pallas_call(functools.partial(kernel, (heads, width, tokens, seq_count...  19.6 us
    unnamed x1, local copies, waits for them, and re-layouts  0.8 us

profile of v4, /device:TPU:0, one launch (start us, length us, event | category | flops | bytes accessed | tf_op | source)
XLA Modules:
  0.0 20.4 jit_solution(15234905367991175149)
XLA Ops:
  0.0 19.6 %shard_map.55 = bf16[128,2048]{1,0:T(8,128)(2,1)S(1)} custom-call(bf16[128,2048]{1,0:T(8,128)(2,1)} %bitcast.5, bf16[128,2048]{1,0:T(8,128)(2,1)} %bitcast.6, bf16[128,2048]{1,0:T(8,128)(2,1)} %bitcast.7, s32[1,2048]{1,0:T(1,128)} %refs_3_.1, s32[32]{0:T(128)} %refs_4_.1), custom_call_target="tpu_custom_call" | custom-call | tf_op jit(solution)/shard_map/pallas_call | solution.py:658
  19.6 0.8 %copy.7 = bf16[2,64,2048]{2,1,0:T(8,128)(2,1)} copy(bf16[2,64,2048]{2,1,0:T(8,128)(2,1)S(1)} %bitcast.4) | data formatting | bytes 1048576

commit v5 on v4

--- a/solution.py
+++ b/solution.py
@@ -174,10 +174,9 @@
     def leaf_bias(count):
         return jnp.where(iota((LEAF, LANES), 0) < count, 0.0, NEG)
 
-    def permute(m):
-        for p in range(2):
-            n = 2 * m + p
-            at = pl.multiple_of(n * LEAF, LEAF)
+    def permute(group):
+        for n in group:
+            at = n * LEAF
             picks = order[0:1, pl.ds(at, LEAF)]
             spots = iota((tokens, LEAF), 0)
             hot = jnp.where(spots == picks, 1.0, 0.0).astype(BF)
@@ -241,10 +240,10 @@
     def pool_far(m):
         if not pieced:
             return
-        start = pl.multiple_of(m * 2 * LEAF, 2 * LEAF)
+        start = m * 2 * LEAF
         kk = []
         for p in range(2):
-            at = pl.multiple_of(start + p * LEAF, LEAF)
+            at = start + p * LEAF
             kk.append(dot(uf[...], kv[pl.ds(at, LEAF), rows:]))
         for level in pieced:
             count = LEAF >> level
@@ -258,10 +257,10 @@
             fp[level][m, :, rows:] = fixed(x[:, rows:], BOUND * 2**level)
 
     def pool_near(m):
-        start = pl.multiple_of(m * 2 * LEAF, 2 * LEAF)
+        start = m * 2 * LEAF
         t1, kk = [], []
         for p in range(2):
-            at = pl.multiple_of(start + p * LEAF, LEAF)
+            at = start + p * LEAF
             t1.append(dot(xp[0 : 2 * rows, pl.ds(at, LEAF)], w1[p]))
             kk.append(dot(ua[...], kv[pl.ds(at, LEAF), 0 : 2 * rows]))
         if far_levels:
@@ -276,7 +275,7 @@
         if 2 in near_levels:
             b2 = base_of[2] + m // 2
             x2 = t1[0][:, LANES:] + t1[1][:, LANES:]
-            where = pl.ds(pl.multiple_of((m % 2) * LANES, LANES), LANES)
+            where = pl.ds((m % 2) * LANES, LANES)
             mass = jnp.where(
                 lane < 64, clip_mass(n[0], lane << 2, 4), clip_mass(n[1], (lane - 64) << 2, 4)
             )
@@ -293,7 +292,7 @@
                 if level == 1:
                     put_key(kmf.at[b1], a, b, bias, slice(p * count, (p + 1) * count))
                 else:
-                    spot = pl.multiple_of((m % 2) * LANES + p * count, count)
+                    spot = (m % 2) * LANES + p * count
                     put_key(kmf.at[b2], a, b, bias, pl.ds(spot, count))
 
     def remote(src, dst, send, recv, target):
@@ -326,9 +325,6 @@
             ),
         )
 
-    def pair_at(i):
-        return jnp.where(i == 0, 0, jnp.where(i == 1, pairs - 1, i - 1))
-
     def far_copies(level, piece):
         bit = level - depth_local
         nb = 1 << bit
@@ -346,35 +342,37 @@
             for j in range(nb)
         ]
 
-    permute(0)
-
-    @pl.loop(1, pairs)
-    def _(i):
-        pool_far(pair_at(i - 1))
-        permute(pair_at(i))
-
-        @pl.when(i == 1)
-        def _():
+    def send_far(m):
+        for level in reversed(pieced):
+            for copy in far_copies(level, m):
+                copy.start()
+
+    groups = [(0, leaves - 1), (1, leaves - 2)] + [(2 * m, 2 * m + 1) for m in range(1, pairs - 1)]
+    ready = [[], []] + [[0, pairs - 1]] + [[m] for m in range(1, pairs - 1)]
+    for step, group in enumerate(groups):
+        for m in ready[step]:
+            pool_far(m)
+        permute(group)
+        if step == 0:
             pl.semaphore_wait(barrier, seq_count - 1)
 
-        @pl.when(jnp.logical_and(i == 1, has_left))
-        def _():
-            for copy in halo(0):
-                copy.start()
-
-        @pl.when(jnp.logical_and(i == 1, has_right))
-        def _():
-            for copy in halo(1):
-                copy.start()
-
-        for level in reversed(pieced):
-            for copy in far_copies(level, pair_at(i - 1)):
-                copy.start()
-
-    pool_far(pair_at(pairs - 1))
-    for level in reversed(pieced):
-        for copy in far_copies(level, pair_at(pairs - 1)):
-            copy.start()
+            @pl.when(has_left)
+            def _():
+                for copy in halo(0):
+                    copy.start()
+
+            @pl.when(has_right)
+            def _():
+                for copy in halo(1):
+                    copy.start()
+
+        for m in ready[step]:
+            send_far(m)
+    for m in ready[len(groups)]:
+        pool_far(m)
+    pool_near(0)
+    for m in ready[len(groups)]:
+        send_far(m)
     for level in us:
         sums = dot(us[level][...], kv[:, rows:])
         valid = jnp.broadcast_to(xp[2 * rows : 2 * rows + 1, :], (LANES, tokens))
@@ -384,8 +382,7 @@
         for copy in far_copies(level, 0):
             copy.start()
 
-    @pl.loop(0, pairs, unroll=2)
-    def _(m):
+    for m in range(1, pairs):
         pool_near(m)
 
     for i, level in enumerate(far_levels):
@@ -425,32 +422,6 @@
 
     def local_soft(i, slot, h):
         far_soft([vvf[i ^ 1, h]], slot, h, fb.at[i], fo.at[i])
-
-    for h in range(heads):
-        local_score(0, 0, h)
-
-    @pl.loop(0, first // 2)
-    def _(b):
-        for j in range(2):
-            i = 2 * b + j
-            for h in range(heads):
-                local_soft(i, j, h)
-                local_score(jnp.minimum(i + 1, first - 1), 1 - j, h)
-
-    @pl.when(has_right)
-    def _():
-        for copy in halo(0):
-            copy.wait_recv()
-
-    @pl.when(has_left)
-    def _():
-        for copy in halo(1):
-            copy.wait_recv()
-
-    for n, at in ((-1, 0), (leaves, tokens + LEAF)):
-        tail0, tail1, _ = key_tail(ka[at : at + LEAF, :].astype(F32), leaf_bias(count_of(n)))
-        kb[0, at : at + LEAF, :] = tail0.astype(BF)
-        kb[1, at : at + LEAF, :] = tail1.astype(BF)
 
     def near_score(n, slot, h):
         at = pl.multiple_of(n * LEAF, LEAF)
@@ -481,16 +452,45 @@
         stat[2 * h : 2 * h + 1, pl.ds(at, LEAF)] = best[0:1]
         stat[2 * h + 1 : 2 * h + 2, pl.ds(at, LEAF)] = jnp.sum(total, axis=0, keepdims=True)
 
+    def leaf_at(k):
+        return jnp.where(k < leaves - 2, k + 1, jnp.where(k == leaves - 2, 0, leaves - 1))
+
     for h in range(heads):
-        near_score(0, 0, h)
+        local_score(0, 0, h)
+    for i in range(first):
+        for h in range(heads):
+            local_soft(i, i % 2, h)
+            if i + 1 < first:
+                local_score(i + 1, 1 - i % 2, h)
+            else:
+                near_score(leaf_at(0), 1 - i % 2, h)
+    turn = first % 2
 
     @pl.loop(0, leaves // 4)
     def _(i):
+        @pl.when(jnp.logical_and(i == 1, has_right))
+        def _():
+            for copy in halo(0):
+                copy.wait_recv()
+
+        @pl.when(jnp.logical_and(i == 1, has_left))
+        def _():
+            for copy in halo(1):
+                copy.wait_recv()
+
+        @pl.when(i == 1)
+        def _():
+            for n, at in ((-1, 0), (leaves, tokens + LEAF)):
+                tail0, tail1, _ = key_tail(ka[at : at + LEAF, :].astype(F32), leaf_bias(count_of(n)))
+                kb[0, at : at + LEAF, :] = tail0.astype(BF)
+                kb[1, at : at + LEAF, :] = tail1.astype(BF)
+
         for j in range(4):
-            n = 4 * i + j
+            k = 4 * i + j
+            slot = (turn + j) % 2
             for h in range(heads):
-                near_soft(n, j % 2, h)
-                near_score(jnp.minimum(n + 1, leaves - 1), 1 - j % 2, h)
+                near_soft(leaf_at(k), slot, h)
+                near_score(leaf_at(jnp.minimum(k + 1, leaves - 1)), 1 - slot, h)
 
     for level in reversed(far_levels):
         pieces = fp[level].shape[0]

time: 20.5 us -> 19.2 us (0.937)
  Pallas kernels: 19.6 us -> 18.3 us
    pallas_call x1, Pallas kernels: 19.6 us -> 18.3 us  [shards(): pl.pallas_call(functools.partial(kernel, (heads, width, tokens, seq_count...]
where the time goes in v5:
time: 19.2 us; the launch traced here: 19.1 us
  Pallas kernels  18.3 us (95%)
  local copies, waits for them, and re-layouts  0.8 us (4%)
    pallas_call x1, Pallas kernels, shards(): pl.pallas_call(functools.partial(kernel, (heads, width, tokens, seq_count...  18.3 us
    unnamed x1, local copies, waits for them, and re-layouts  0.8 us

profile of v5, /device:TPU:0, one launch (start us, length us, event | category | flops | bytes accessed | tf_op | source)
XLA Modules:
  0.0 19.1 jit_solution(15261302608727330512)
XLA Ops:
  0.0 18.3 %shard_map.55 = bf16[128,2048]{1,0:T(8,128)(2,1)S(1)} custom-call(bf16[128,2048]{1,0:T(8,128)(2,1)} %bitcast.5, bf16[128,2048]{1,0:T(8,128)(2,1)} %bitcast.6, bf16[128,2048]{1,0:T(8,128)(2,1)} %bitcast.7, s32[1,2048]{1,0:T(1,128)} %refs_3_.1, s32[32]{0:T(128)} %refs_4_.1), custom_call_target="tpu_custom_call" | custom-call | tf_op jit(solution)/shard_map/pallas_call | solution.py:658
  18.3 0.8 %copy.7 = bf16[2,64,2048]{2,1,0:T(8,128)(2,1)} copy(bf16[2,64,2048]{2,1,0:T(8,128)(2,1)S(1)} %bitcast.4) | data formatting | bytes 1048576

commit v6 on v5

--- a/solution.py
+++ b/solution.py
@@ -116,48 +116,51 @@
     def ones_where(mask):
         return jnp.where(mask, 1.0, 0.0).astype(BF)
 
-    t = iota((LEAF, LEAF), 0)
-    c = iota((LEAF, LEAF), 1)
-    for p in range(2):
-        w1[p] = ones_where(
-            jnp.logical_or(
-                jnp.logical_and(c < LANES, (t >> 1) == c),
-                jnp.logical_and(c >= LANES, (t >> 2) + 64 * p == c - LANES),
+    ua_at, uf_at = {}, {}
+
+    def constants():
+        t = iota((LEAF, LEAF), 0)
+        c = iota((LEAF, LEAF), 1)
+        for p in range(2):
+            w1[p] = ones_where(
+                jnp.logical_or(
+                    jnp.logical_and(c < LANES, (t >> 1) == c),
+                    jnp.logical_and(c >= LANES, (t >> 2) + 64 * p == c - LANES),
+                )
             )
-        )
-    uu[...] = ones_where((c >> 1) == (t & (LANES - 1)))
-    for i, level in enumerate(far_levels):
-        t2 = iota((2 * LEAF, LANES), 0)
-        c2 = iota((2 * LEAF, LANES), 1)
-        for m in range(pairs):
-            w3[m, :, i * LANES : (i + 1) * LANES] = ones_where(
-                ((t2 + 2 * LEAF * m) >> level) & (LANES - 1) == c2
-            )
-    ua_at, uf_at = {}, {}
-    for ref, spots, which in ((ua, ua_at, near_levels), (uf, uf_at, pieced)):
-        at = 0
-        for level in which:
-            n = max(LEAF >> level, 16)
-            spots[level] = at
-            ref[at : at + n, :] = ones_where((iota((n, LEAF), 1) >> level) == iota((n, LEAF), 0))
-            at += n
-    for level, u in us.items():
-        u[...] = ones_where((iota(u.shape, 1) >> level) == iota(u.shape, 0))
-
-    def tail_rows(cols):
-        r = iota((64, cols), 0)
-        return ones_where(r == 0)
-
-    for h in range(heads):
-        off = (1 - h) * width
-        qx[h, off : off + width, :] = jnp.zeros((width, tokens), BF)
-        qx[h, 3 * width :, :] = tail_rows(tokens)
-        for i in range(qf.shape[0]):
-            qf[i, h, 3 * width :, :] = tail_rows(LEAF)
-        for level in far_levels:
-            qr[level][h, 3 * width :, :] = tail_rows(qr[level].shape[2])
-
-    for load in loads:
+        uu[...] = ones_where((c >> 1) == (t & (LANES - 1)))
+        for i, level in enumerate(far_levels):
+            t2 = iota((2 * LEAF, LANES), 0)
+            c2 = iota((2 * LEAF, LANES), 1)
+            for m in range(pairs):
+                w3[m, :, i * LANES : (i + 1) * LANES] = ones_where(
+                    ((t2 + 2 * LEAF * m) >> level) & (LANES - 1) == c2
+                )
+        for ref, spots, which in ((ua, ua_at, near_levels), (uf, uf_at, pieced)):
+            at = 0
+            for level in which:
+                n = max(LEAF >> level, 16)
+                spots[level] = at
+                ref[at : at + n, :] = ones_where((iota((n, LEAF), 1) >> level) == iota((n, LEAF), 0))
+                at += n
+        for level, u in us.items():
+            u[...] = ones_where((iota(u.shape, 1) >> level) == iota(u.shape, 0))
+
+        def tail_rows(cols):
+            r = iota((64, cols), 0)
+            return ones_where(r == 0)
+
+        for h in range(heads):
+            off = (1 - h) * width
+            qx[h, off : off + width, :] = jnp.zeros((width, tokens), BF)
+            qx[h, 3 * width :, :] = tail_rows(tokens)
+            for i in range(qf.shape[0]):
+                qf[i, h, 3 * width :, :] = tail_rows(LEAF)
+            for level in far_levels:
+                qr[level][h, 3 * width :, :] = tail_rows(qr[level].shape[2])
+
+    constants()
+    for load in loads[1:]:
         load.wait()
 
     lane_lo = iota((LEAF, LANES), 1) < width
@@ -174,34 +177,41 @@
     def leaf_bias(count):
         return jnp.where(iota((LEAF, LANES), 0) < count, 0.0, NEG)
 
-    def permute(group):
+    def put_keys(n, key, value):
+        at = n * LEAF
+        count = count_of(n)
+        key_t = key.T
+        on_row = iota((rows, LEAF), 1) < count
+        on_col = iota((LEAF, rows), 0) < count
+        tail0, tail1, rolled = key_tail(key_t, leaf_bias(count))
+        ka[at + LEAF : at + 2 * LEAF, :] = key_t.astype(BF)
+        kb[0, at + LEAF : at + 2 * LEAF, :] = tail0.astype(BF)
+        kb[1, at + LEAF : at + 2 * LEAF, :] = tail1.astype(BF)
+        kv[at : at + LEAF, 0:rows] = jnp.where(on_col, rolled, 0.0).astype(BF)
+        kv[at : at + LEAF, rows : 2 * rows] = jnp.where(on_col, key_t, 0.0).astype(BF)
+        kv[at : at + LEAF, 2 * rows :] = jnp.where(on_col, value.T, 0.0).astype(BF)
+        vx[:, at + LEAF : at + 2 * LEAF] = value.astype(BF)
+        xp[rows : 2 * rows, at : at + LEAF] = jnp.where(on_row, value, 0.0).astype(BF)
+        xp[2 * rows :, at : at + LEAF] = ones_where(on_row[:PAD])
+
+    def put_queries(n, query):
+        cols = slice(n * LEAF, (n + 1) * LEAF)
+        xp[0:rows, cols] = query.astype(BF)
+        hi, lo = split(query * scale)
+        for h in range(heads):
+            part = slice(h * width, (h + 1) * width)
+            qx[h, part, cols] = hi[part]
+            qx[h, 2 * width : 3 * width, cols] = lo[part]
+
+    def permute(group, start=0, stop=3):
         for n in group:
-            at = n * LEAF
-            picks = order[0:1, pl.ds(at, LEAF)]
-            spots = iota((tokens, LEAF), 0)
-            hot = jnp.where(spots == picks, 1.0, 0.0).astype(BF)
-            moved = dot(xin[...], hot)
-            count = count_of(n)
-            query, key, value = moved[:rows], moved[rows : 2 * rows], moved[2 * rows :]
-            key_t = key.T
-            on_row = iota((rows, LEAF), 1) < count
-            on_col = iota((LEAF, rows), 0) < count
-            tail0, tail1, rolled = key_tail(key_t, leaf_bias(count))
-            ka[pl.ds(at + LEAF, LEAF), :] = key_t.astype(BF)
-            kb[0, pl.ds(at + LEAF, LEAF), :] = tail0.astype(BF)
-            kb[1, pl.ds(at + LEAF, LEAF), :] = tail1.astype(BF)
-            kv[pl.ds(at, LEAF), 0:rows] = jnp.where(on_col, rolled, 0.0).astype(BF)
-            kv[pl.ds(at, LEAF), rows : 2 * rows] = jnp.where(on_col, key_t, 0.0).astype(BF)
-            kv[pl.ds(at, LEAF), 2 * rows :] = jnp.where(on_col, value.T, 0.0).astype(BF)
-            vx[:, pl.ds(at + LEAF, LEAF)] = value.astype(BF)
-            xp[0:rows, pl.ds(at, LEAF)] = query.astype(BF)
-            xp[rows : 2 * rows, pl.ds(at, LEAF)] = jnp.where(on_row, value, 0.0).astype(BF)
-            xp[2 * rows :, pl.ds(at, LEAF)] = ones_where(on_row[:PAD])
-            hi, lo = split(query * scale)
-            for h in range(heads):
-                part = slice(h * width, (h + 1) * width)
-                qx[h, part, pl.ds(at, LEAF)] = hi[part]
-                qx[h, 2 * width : 3 * width, pl.ds(at, LEAF)] = lo[part]
+            picks = order[0:1, n * LEAF : (n + 1) * LEAF]
+            hot = jnp.where(iota((tokens, LEAF), 0) == picks, 1.0, 0.0).astype(BF)
+            moved = dot(xin[start * rows : stop * rows], hot)
+            if start == 0:
+                put_queries(n, moved[:rows])
+            if stop == 3:
+                put_keys(n, moved[(1 - start) * rows : (2 - start) * rows], moved[(2 - start) * rows :])
 
     def put_query(ref, x, factor, where):
         hi, lo = split(x * factor)
@@ -352,8 +362,10 @@
     for step, group in enumerate(groups):
         for m in ready[step]:
             pool_far(m)
-        permute(group)
-        if step == 0:
+        if step:
+            permute(group)
+        else:
+            permute(group, start=1)
             pl.semaphore_wait(barrier, seq_count - 1)
 
             @pl.when(has_left)
@@ -366,11 +378,14 @@
                 for copy in halo(1):
                     copy.start()
 
+            loads[0].wait()
+
         for m in ready[step]:
             send_far(m)
     for m in ready[len(groups)]:
         pool_far(m)
-    pool_near(0)
+    if pairs > 2:
+        pool_near(1)
     for m in ready[len(groups)]:
         send_far(m)
     for level in us:
@@ -382,7 +397,10 @@
         for copy in far_copies(level, 0):
             copy.start()
 
-    for m in range(1, pairs):
+    for m in range(2, pairs - 1):
+        pool_near(m)
+    permute(groups[0], stop=1)
+    for m in (0, pairs - 1):
         pool_near(m)
 
     for i, level in enumerate(far_levels):

time: 19.2 us -> 19 us (0.990)
  Pallas kernels: 18.3 us -> 18 us
    pallas_call x1, Pallas kernels: 18.3 us -> 18 us  [shards(): pl.pallas_call(functools.partial(kernel, (heads, width, tokens, seq_count...]
where the time goes in v6:
time: 19 us; the launch traced here: 18.8 us
  Pallas kernels  18 us (95%)
  local copies, waits for them, and re-layouts  0.8 us (4%)
    pallas_call x1, Pallas kernels, shards(): pl.pallas_call(functools.partial(kernel, (heads, width, tokens, seq_count...  18 us
    unnamed x1, local copies, waits for them, and re-layouts  0.8 us

profile of v6, /device:TPU:0, one launch (start us, length us, event | category | flops | bytes accessed | tf_op | source)
XLA Modules:
  0.0 18.8 jit_solution(5039055893331084844)
XLA Ops:
  0.0 18.0 %shard_map.55 = bf16[128,2048]{1,0:T(8,128)(2,1)S(1)} custom-call(bf16[128,2048]{1,0:T(8,128)(2,1)} %bitcast.5, bf16[128,2048]{1,0:T(8,128)(2,1)} %bitcast.6, bf16[128,2048]{1,0:T(8,128)(2,1)} %bitcast.7, s32[1,2048]{1,0:T(1,128)} %refs_3_.1, s32[32]{0:T(128)} %refs_4_.1), custom_call_target="tpu_custom_call" | custom-call | tf_op jit(solution)/shard_map/pallas_call | solution.py:676
  18.0 0.8 %copy.7 = bf16[2,64,2048]{2,1,0:T(8,128)(2,1)} copy(bf16[2,64,2048]{2,1,0:T(8,128)(2,1)S(1)} %bitcast.4) | data formatting | bytes 1048576

commit v7 on v6

--- a/solution.py
+++ b/solution.py
@@ -384,10 +384,10 @@
             send_far(m)
     for m in ready[len(groups)]:
         pool_far(m)
+    for m in ready[len(groups)]:
+        send_far(m)
     if pairs > 2:
         pool_near(1)
-    for m in ready[len(groups)]:
-        send_far(m)
     for level in us:
         sums = dot(us[level][...], kv[:, rows:])
         valid = jnp.broadcast_to(xp[2 * rows : 2 * rows + 1, :], (LANES, tokens))

time: 19 us -> 19 us (level)
  no operation moved by 1% of the time
where the time goes in v7:
time: 19 us; the launch traced here: 18.8 us
  Pallas kernels  18 us (95%)
  local copies, waits for them, and re-layouts  0.8 us (4%)
    pallas_call x1, Pallas kernels, shards(): pl.pallas_call(functools.partial(kernel, (heads, width, tokens, seq_count...  18 us
    unnamed x1, local copies, waits for them, and re-layouts  0.8 us

profile of v7, /device:TPU:0, one launch (start us, length us, event | category | flops | bytes accessed | tf_op | source)
XLA Modules:
  0.0 18.8 jit_solution(7316254321796755147)
XLA Ops:
  0.0 18.0 %shard_map.55 = bf16[128,2048]{1,0:T(8,128)(2,1)S(1)} custom-call(bf16[128,2048]{1,0:T(8,128)(2,1)} %bitcast.5, bf16[128,2048]{1,0:T(8,128)(2,1)} %bitcast.6, bf16[128,2048]{1,0:T(8,128)(2,1)} %bitcast.7, s32[1,2048]{1,0:T(1,128)} %refs_3_.1, s32[32]{0:T(128)} %refs_4_.1), custom_call_target="tpu_custom_call" | custom-call | tf_op jit(solution)/shard_map/pallas_call | solution.py:676
  18.1 0.8 %copy.7 = bf16[2,64,2048]{2,1,0:T(8,128)(2,1)} copy(bf16[2,64,2048]{2,1,0:T(8,128)(2,1)S(1)} %bitcast.4) | data formatting | bytes 1048576
